TPU v7x, 256 devices: a whole 4x4x8 slice. The times are simulated.
256 devices in a mesh: expert: 16 (over x_hi, y, core), dp: 16 (over x_lo, z).
Axes of the slice: x: 4 (x_hi: 2, x_lo: 2; x = x_hi * 2 + x_lo), y: 4, z: 8, core: 2. Of those that a mesh axis runs over, the one named last changes fastest.
Arguments:
- cotangent: bfloat16 [32768, 2048], P(('expert', 'dp')), may hold values from -6 to 6
- hidden: bfloat16 [32768, 7168], P(('expert', 'dp')), may hold values from -0.1796875 to 0.1796875
- codes: bfloat16 [16, 7168, 1024], P('expert', 'dp'), may hold values from -0.125 to 0.125
- scales: float32 [16, 7168], P('expert', 'dp'), may hold values from 0.3 to 3
- counts: int32 [256, 8], replicated, may hold values from 0 to 24, as said below
Outputs:
- d_hidden: bfloat16 [32768, 7168], P(('expert', 'dp'))
- weight_grad: float32 [16, 7168, 1024], P('expert', 'dp')
Inputs may be any that keep to these rules, and one draw needn't show every extreme that they name: Row p of counts is device p's split of its 128 rows over the experts, devices numbered with the expert index first; a device's rows are grouped by expert in increasing order. Each row sums to 128 and has an entry equal to 24. In every draw all devices of one pair of neighbouring expert indices give their 24 rows to the same expert.
All inputs are finite; a program needn't handle non-finite values.
Results may differ from a plain program's by a relative error of at most 0.001.
Values may be sent and summed in bfloat16 or wider, within the bound.
No kernel may reach another device: no remote copies, remote signals or barrier semaphores. Data moves between devices by JAX's collectives and lax.ppermute only.
A program may use at most 192 MiB of HBM per device.

v0:
```python
import jax
import jax.numpy as jnp
from jax import lax
from jax.experimental import pallas as pl
from jax.experimental.pallas import tpu as pltpu
from jax.sharding import Mesh, PartitionSpec as P

PLACES = ("xh", "y")
SWAP = [(0, 1), (1, 0)]


def slot_hot(row_counts, slots, rows):
    starts = jnp.cumsum(row_counts, axis=-1) - row_counts
    slot = jnp.arange(slots, dtype=jnp.int32)
    source = jnp.where(slot < row_counts[..., None], starts[..., None] + slot, -1)
    return (source[..., None] == jnp.arange(rows, dtype=jnp.int32)).astype(jnp.bfloat16)


def distances(depth):
    order = [depth // 2]
    for k in range(depth // 2 - 1, 0, -1):
        order += [k, -k]
    return order + [0]


def after(value, *others):
    return lax.optimization_barrier((value,) + others)[0]


def along_z(value, by):
    depth = lax.axis_size("z")
    return lax.ppermute(value, "z", [(i, (i + by) % depth) for i in range(depth)])


def split_kernel(level_ref, hidden_ref, *refs):
    outs, held = refs[:-1], refs[-1]
    depth, _, wide = held.shape
    share = wide // 2
    for z in range(depth):
        low = hidden_ref[:, z * share : (z + 1) * share]
        high = hidden_ref[:, (depth + z) * share : (depth + z + 1) * share]
        held[z] = jnp.concatenate([low, high], axis=1)
    for out, by in zip(outs, distances(depth)):
        out[...] = held[lax.rem(level_ref[0] + (by + depth), depth)]


def split_levels(hidden, level, depth):
    rows, width = hidden.shape
    block = (rows, width // depth)
    whole = pl.BlockSpec(memory_space=pltpu.VMEM)
    return pl.pallas_call(
        split_kernel,
        out_shape=[jax.ShapeDtypeStruct(block, hidden.dtype)] * depth,
        in_specs=[pl.BlockSpec(memory_space=pltpu.SMEM), whole],
        out_specs=[whole] * depth,
        scratch_shapes=[pltpu.VMEM((depth,) + block, hidden.dtype)],
        compiler_params=pltpu.CompilerParams(vmem_limit_bytes=40 << 20),
    )(level, hidden)


def join_kernel(level_ref, *refs):
    parts, out_ref, held = refs[:-2], refs[-2], refs[-1]
    depth, _, wide = held.shape
    share = wide // 2
    for part, by in zip(parts, distances(depth)):
        held[lax.rem(level_ref[0] + (by + depth), depth)] = part[...]
    for z in range(0, depth, 2):
        for s in range(2):
            pair = [held[z + i, :, s * share : (s + 1) * share] for i in range(2)]
            out_ref[:, (s * depth + z) * share : (s * depth + z + 2) * share] = (
                jnp.concatenate(pair, axis=1)
            )


def join_levels(parts, level):
    depth = len(parts)
    rows, wide = parts[0].shape
    whole = pl.BlockSpec(memory_space=pltpu.VMEM)
    return pl.pallas_call(
        join_kernel,
        out_shape=jax.ShapeDtypeStruct((rows, depth * wide), parts[0].dtype),
        in_specs=[pl.BlockSpec(memory_space=pltpu.SMEM)] + [whole] * depth,
        out_specs=whole,
        scratch_shapes=[pltpu.VMEM((depth, rows, wide), parts[0].dtype)],
        compiler_params=pltpu.CompilerParams(vmem_limit_bytes=40 << 20),
    )(level, *parts)


def halves_of(ref, core, half):
    own = pl.multiple_of(core * half, half)
    return ref[..., pl.ds(own, half)], ref[..., pl.ds(pl.multiple_of(half - own, half), half)]


def join_rows_kernel(place_ref, core_ref, next_ref, own_ref, mate_ref, own_scales, mate_scales, *refs):
    rows_refs, out_ref, passed_ref = refs[:-2], refs[-2], refs[-1]
    for i in range(next_ref.shape[0]):
        passed_ref[i] = next_ref[i]
    half = own_ref.shape[0]
    pairs = [halves_of(ref, core_ref[0], half) for ref in rows_refs]
    own = jnp.concatenate([pair[0][0] for pair in pairs])
    mate = jnp.concatenate([pair[1][0] for pair in pairs])
    total = own_scales[...] * jnp.dot(own, own_ref[...], preferred_element_type=jnp.float32)
    total += mate_scales[...] * jnp.dot(mate, mate_ref[...], preferred_element_type=jnp.float32)
    places, steps, slots, wide = out_ref.shape
    total = total.reshape(steps, places, slots, wide).astype(out_ref.dtype)
    for step in range(steps):
        out_ref[:, step] = total[step]


def join_rows(where, core, then, values, codes, scales, places):
    steps = where.shape[0]
    _, rows, cols = values.shape
    half, wide = codes[0].shape

    def rows_spec(j):
        return pl.BlockSpec((1, rows, cols), lambda i, w, c: (w[j], 0, 0))

    def whole(*shape):
        return pl.BlockSpec(shape, lambda i, w, c: (0,) * len(shape))

    words = pl.BlockSpec(memory_space=pltpu.SMEM)
    shape = (places, steps, rows // places, wide)
    return pl.pallas_call(
        join_rows_kernel,
        out_shape=[pltpu.HBM(shape, jnp.bfloat16), jax.ShapeDtypeStruct(then.shape, then.dtype)],
        grid_spec=pltpu.PrefetchScalarGridSpec(
            num_scalar_prefetch=2,
            grid=(1,),
            in_specs=[words] + [whole(half, wide)] * 2 + [whole(1, wide)] * 2
            + [rows_spec(j) for j in range(steps)],
            out_specs=[whole(*shape), words],
        ),
        compiler_params=pltpu.CompilerParams(vmem_limit_bytes=40 << 20),
    )(where, core, then, *codes, *scales, *[values] * steps)


def weight_kernel(core_ref, values_ref, mate_values_ref, own_ref, mate_ref, out_ref):
    half = out_ref.shape[1]
    own_rows = halves_of(values_ref, core_ref[0], half)[0].reshape(-1, half)
    mate_rows = halves_of(mate_values_ref, core_ref[0], half)[0].reshape(-1, half)
    part = lax.dot_general(
        jnp.concatenate([own_ref[...], mate_ref[...]]),
        jnp.concatenate([own_rows, mate_rows]),
        (((0,), (0,)), ((), ())),
        preferred_element_type=jnp.float32,
    )

    @pl.when(pl.program_id(0) == 0)
    def _():
        out_ref[...] = part

    @pl.when(pl.program_id(0) > 0)
    def _():
        out_ref[...] += part


def weight_sums(core, values, mate_values, own, mate, levels=2):
    depth, rows, cols = values.shape
    wide, half = own.shape[1], cols // 2
    units = pl.BlockSpec((levels * rows, wide), lambda i, c: (i, 0))
    return pl.pallas_call(
        weight_kernel,
        out_shape=pltpu.HBM((wide, half), jnp.float32),
        grid_spec=pltpu.PrefetchScalarGridSpec(
            num_scalar_prefetch=1,
            grid=(depth // levels,),
            in_specs=[
                pl.BlockSpec((levels, rows, cols), lambda i, c: (i, 0, 0)),
                pl.BlockSpec((levels, rows, cols), lambda i, c: (i, 0, 0)),
                units,
                units,
            ],
            out_specs=pl.BlockSpec((wide, half), lambda i, c: (0, 0)),
        ),
        compiler_params=pltpu.CompilerParams(vmem_limit_bytes=40 << 20),
    )(core, values, mate_values, own, mate)


def rows_kernel(counts_ref, rows_ref, out_ref):
    experts, slots, cols = out_ref.shape
    rows = rows_ref.shape[0]
    slot = lax.broadcasted_iota(jnp.int32, (slots, rows), 0)
    row = lax.broadcasted_iota(jnp.int32, (slots, rows), 1)
    hot, start = [], 0
    for e in range(experts):
        count = counts_ref[e]
        hit = jnp.logical_and(row == slot + start, slot < count)
        hot.append(jnp.where(hit, 1.0, 0.0))
        start = start + count
    hot = jnp.concatenate(hot).astype(jnp.bfloat16)
    packed = jnp.dot(hot, rows_ref[...], preferred_element_type=jnp.float32)
    out_ref[...] = packed.reshape(experts, slots, cols).astype(out_ref.dtype)


def pack_rows(counts, cotangent, slots):
    rows, cols = cotangent.shape
    whole = pl.BlockSpec(memory_space=pltpu.VMEM)
    return pl.pallas_call(
        rows_kernel,
        out_shape=jax.ShapeDtypeStruct((counts.shape[0], slots, cols), cotangent.dtype),
        in_specs=[pl.BlockSpec(memory_space=pltpu.SMEM), whole],
        out_specs=whole,
        compiler_params=pltpu.CompilerParams(vmem_limit_bytes=40 << 20),
    )(counts, cotangent)


def unpack_kernel(hot_ref, back_ref, *outs):
    experts, _, slots, wide = back_ref.shape
    for i, out in enumerate(outs):
        packed = back_ref[:, i].astype(jnp.float32).reshape(experts * slots, wide)
        out[...] = lax.dot_general(
            hot_ref[i], packed.astype(jnp.bfloat16), (((0,), (0,)), ((), ())),
            preferred_element_type=jnp.float32,
        ).astype(out.dtype)


def unpack(hot, back):
    steps, _, rows = hot.shape
    whole = pl.BlockSpec(memory_space=pltpu.VMEM)
    return pl.pallas_call(
        unpack_kernel,
        out_shape=[jax.ShapeDtypeStruct((rows, back.shape[-1]), back.dtype)] * steps,
        in_specs=[whole, whole],
        out_specs=[whole] * steps,
        compiler_params=pltpu.CompilerParams(vmem_limit_bytes=40 << 20),
    )(hot, back)


def pack_kernel(level_ref, hot_ref, *refs):
    blocks, out_ref = refs[:-1], refs[-1]
    experts, depth, slots, wide = out_ref.shape
    for i, by in enumerate(distances(depth)):
        packed = jnp.dot(hot_ref[i], blocks[i][...], preferred_element_type=jnp.float32)
        level = lax.rem(level_ref[0] + (by + depth), depth)
        out_ref[:, level] = packed.reshape(experts, slots, wide).astype(out_ref.dtype)


def pack_hidden(hot, blocks, level, experts):
    depth, places, rows = hot.shape
    wide = blocks[0].shape[1]
    whole = pl.BlockSpec(memory_space=pltpu.VMEM)
    return pl.pallas_call(
        pack_kernel,
        out_shape=pltpu.HBM((experts, depth, places // experts, wide), jnp.bfloat16),
        in_specs=[pl.BlockSpec(memory_space=pltpu.SMEM)] + [whole] * (depth + 1),
        out_specs=whole,
        compiler_params=pltpu.CompilerParams(vmem_limit_bytes=40 << 20),
    )(level, hot, *blocks)


def shards(cotangent, hidden, codes, scales, counts):
    rows, cols = cotangent.shape
    half = cols // 2
    share = codes.shape[1]
    places = lax.axis_size(PLACES)
    depth = lax.axis_size("z")
    experts = counts.shape[1]
    slots = 3 * rows // (2 * experts)
    wide = 2 * share
    order = distances(depth)
    place, core = lax.axis_index(PLACES), lax.axis_index("c")
    side, level = lax.axis_index("xl"), lax.axis_index("z")
    core_word = core.astype(jnp.int32).reshape(1)
    level_word = level.astype(jnp.int32).reshape(1)

    def levels_at(steps):
        return (level.astype(jnp.int32) + jnp.array(steps, jnp.int32) + depth) % depth

    line_at = ((place * 2 + core) * 2 + side) * depth
    own_counts = lax.dynamic_slice_in_dim(counts, line_at + level, 1, 0).reshape(experts)
    line_counts = lax.dynamic_slice_in_dim(counts, line_at, depth, 0)
    near_counts = lax.dynamic_slice_in_dim(jnp.concatenate([line_counts] * 2), level, depth, 0)
    near_counts = jnp.stack([near_counts[by % depth] for by in order])
    near_hot = slot_hot(near_counts, slots, rows).reshape(depth, experts * slots, rows)

    other_codes, other_scales = lax.ppermute((codes[0], scales[0]), "xl", SWAP)
    by_level = split_levels(hidden, level_word, depth)

    packed = pack_rows(own_counts, cotangent, slots)
    arrived = lax.all_to_all(packed, PLACES, 0, 0).reshape(places * slots, cols)

    line_hidden = {}
    for block, by in zip(by_level, order):
        line_hidden[-by if by < depth // 2 else by] = along_z(block, by) if by else block
    arrived, line_hidden[-1], line_hidden[1] = lax.optimization_barrier(
        (arrived, line_hidden[-1], line_hidden[1])
    )
    values = lax.all_gather(arrived, "z", axis=0, tiled=True)
    values = values.reshape(depth, places * slots, cols)

    other_codes, other_scales, *line_hidden = lax.optimization_barrier(
        [other_codes, other_scales] + [line_hidden[by] for by in order]
    )

    hidden_slots = pack_hidden(near_hot, line_hidden, level_word, experts)
    other_codes, other_scales = after((other_codes, other_scales), hidden_slots)
    first = side == 0
    both_codes = jnp.where(first, jnp.stack([codes[0], other_codes]),
                           jnp.stack([other_codes, codes[0]])).reshape(wide, half).T
    both_scales = jnp.where(first, jnp.stack([scales[0], other_scales]),
                            jnp.stack([other_scales, scales[0]])).reshape(1, wide)
    mate_scales, mate_codes = lax.ppermute((both_scales, both_codes), "c", SWAP)

    own_hidden = lax.all_to_all(hidden_slots, PLACES, 0, 0)
    own_hidden = own_hidden.transpose(1, 0, 2, 3).reshape(depth * places * slots, wide)
    mate_hidden = lax.ppermute(own_hidden, "c", SWAP)
    values, mate_codes, mate_scales = lax.optimization_barrier((values, mate_codes, mate_scales))
    values = after(values, own_hidden)
    gathered = values
    values = pltpu.with_memory_space_constraint(values, pltpu.HBM)

    def join(where, then):
        return join_rows(
            where, core_word, then, values, (both_codes, mate_codes), (both_scales, mate_scales), places
        )

    came = {}

    def send_home(steps, back):
        for by, block in zip(steps, back):
            came[-by if by < depth // 2 else by] = along_z(block, by) if by else block

    cut = 3
    far_at, close_at = levels_at(order[:cut]), levels_at(order[cut:])
    far_joined, close_at = join(far_at, close_at)
    close_joined, _ = join(close_at, far_at)
    mate_values = lax.ppermute(gathered, "c", SWAP)
    far_raw = after(lax.all_to_all(far_joined, PLACES, 0, 0), close_joined)
    far_back = unpack(near_hot[:cut], far_raw)
    send_home(order[:cut], far_back)
    own_hidden, mate_hidden = after((own_hidden, mate_hidden), *far_back)
    sums = weight_sums(core_word, values, mate_values, own_hidden, mate_hidden)
    close_raw = after(lax.all_to_all(close_joined, PLACES, 0, 0), *came.values(), sums)
    send_home(order[cut:], unpack(near_hot[cut:], close_raw))

    sums = sums.reshape(2, share, half)
    gone = lax.dynamic_index_in_dim(sums, 1 - side, 0, keepdims=False)
    kept = lax.dynamic_index_in_dim(sums, side, 0, keepdims=False)
    largest = jnp.maximum(jnp.max(jnp.abs(gone)), 1e-30).reshape(1)
    gone = (gone * (1 / largest)).astype(jnp.float16)
    largest = lax.ppermute(largest, "xl", SWAP)
    gone, kept, largest, _ = lax.optimization_barrier((gone, kept, largest, close_raw))
    gone = lax.ppermute(gone, "xl", SWAP)
    weight_grad = kept + gone.astype(jnp.float32) * largest
    d_hidden = join_levels([came[by] for by in order], after(level_word, weight_grad))
    return d_hidden, weight_grad[None]


def solution(mesh):
    lanes, lines = mesh.devices.shape
    fine = Mesh(mesh.devices.reshape(2, lanes // 4, 2, 2, lines // 2), ("xh", "y", "c", "xl", "z"))
    expert, dp = ("xh", "y", "c"), ("xl", "z")
    in_specs = (P(expert + dp, None), P(expert + dp, None), P(expert, dp, None), P(expert, dp), P())
    out_specs = (P(expert + dp, None), P(expert, dp, None))
    return jax.shard_map(shards, mesh=fine, in_specs=in_specs, out_specs=out_specs, check_vma=False)
```

profile of v0, /device:TPU:6, one launch (start us, length us, event | category | flops | bytes accessed | tf_op | source)
XLA Modules:
  0.0 235.7 jit_solution(13399395294427099110)
XLA Ops:
  7.2 0.7 copy-done
  7.9 0.2 dynamic-slice_reduce_fusion.counts_ref
  8.1 1.0 copy-done.5
  9.1 1.8 shard_map.86
  10.9 7.6 %all-to-all-start = ((bf16[8,24,2048]{2,1,0:T(8,128)(2,1)}), bf16[8,24,2048]{2,1,0:T(8,128)(2,1)}, u32[]{:S(2)}, u32[]{:S(2)}) async-start(bf16[8,24,2048]{2,1,0:T(8,128)(2,1)} %shard_map.86), calls=%async_computation | async-start | bytes 1572864 | tf_op jit(solution)/shard_map/all_to_all | solution.py:280
  18.4 0.5 shard_map.87
  18.9 2.0 collective-permute-start
  20.9 4.0 %collective-permute-start.1 = (bf16[128,896]{1,0:T(8,128)(2,1)S(1)}, bf16[128,896]{1,0:T(8,128)(2,1)S(1)}, u32[]{:S(2)}, u32[]{:S(2)}) collective-permute-start(bf16[128,896]{1,0:T(8,128)(2,1)S(1)} %get-tuple-element.49), channel_id=1, source_target_pairs={{0,7},{1,0},{2,1},{3,2},{4,3},{5,4},{6,5},{7,6},{8,15},{9,8},{10,9... | collective-permute-start | bytes 688136 | tf_op jit(solution)/shard_map/ppermute | solution.py:32
  25.0 5.0 %collective-permute-done.refs_6_ = bf16[128,896]{1,0:T(8,128)(2,1)S(1)} collective-permute-done((bf16[128,896]{1,0:T(8,128)(2,1)S(1)}, bf16[128,896]{1,0:T(8,128)(2,1)S(1)}, u32[]{:S(2)}, u32[]{:S(2)}) %collective-permute-start) | collective-permute-done | bytes 229408 | tf_op jit(solution)/shard_map/ppermute | solution.py:32
  30.0 0.9 collective-permute-start.3
  30.9 1.2 collective-permute-start.2
  32.1 7.2 %collective-permute-start.4 = (bf16[128,896]{1,0:T(8,128)(2,1)S(1)}, bf16[128,896]{1,0:T(8,128)(2,1)S(1)}, u32[]{:S(2)}, u32[]{:S(2)}) collective-permute-start(bf16[128,896]{1,0:T(8,128)(2,1)S(1)} %get-tuple-element.51), channel_id=1, source_target_pairs={{0,4},{1,5},{2,6},{3,7},{4,0},{5,1},{6,2},{7,3},{8,12},{9,13},{10,... | collective-permute-start | bytes 688136 | tf_op jit(solution)/shard_map/ppermute | solution.py:32
  39.3 3.8 %collective-permute-start.6 = (bf16[128,896]{1,0:T(8,128)(2,1)S(1)}, bf16[128,896]{1,0:T(8,128)(2,1)S(1)}, u32[]{:S(2)}, u32[]{:S(2)}) collective-permute-start(bf16[128,896]{1,0:T(8,128)(2,1)S(1)} %get-tuple-element.53), channel_id=1, source_target_pairs={{0,3},{1,4},{2,5},{3,6},{4,7},{5,0},{6,1},{7,2},{8,11},{9,12},{10,... | collective-permute-start | bytes 688136 | tf_op jit(solution)/shard_map/ppermute | solution.py:32
  43.2 0.1 pad_add_fusion
  43.4 0.1 fusion.5
  43.4 0.1 stack.23
  43.6 0.1 lt.66
  43.9 0.1 add.89
  44.1 0.9 collective-permute-start.7
  45.1 9.3 %collective-permute-done.4.refs_0_ = bf16[128,896]{1,0:T(8,128)(2,1)S(1)} collective-permute-done((bf16[128,896]{1,0:T(8,128)(2,1)S(1)}, bf16[128,896]{1,0:T(8,128)(2,1)S(1)}, u32[]{:S(2)}, u32[]{:S(2)}) %collective-permute-start.4) | collective-permute-done | bytes 229408 | tf_op jit(solution)/shard_map/ppermute | solution.py:32
  54.3 7.7 %collective-permute-start.8 = (bf16[128,896]{1,0:T(8,128)(2,1)S(1)}, bf16[128,896]{1,0:T(8,128)(2,1)S(1)}, u32[]{:S(2)}, u32[]{:S(2)}) collective-permute-start(bf16[128,896]{1,0:T(8,128)(2,1)S(1)} %get-tuple-element.55), channel_id=1, source_target_pairs={{0,2},{1,3},{2,4},{3,5},{4,6},{5,7},{6,0},{7,1},{8,10},{9,11},{10,... | collective-permute-start | bytes 688136 | tf_op jit(solution)/shard_map/ppermute | solution.py:32
  62.1 0.3 fusion.1.hot_ref
  62.4 13.1 %collective-permute-done.5.refs_1_ = bf16[128,896]{1,0:T(8,128)(2,1)S(1)} collective-permute-done((bf16[128,896]{1,0:T(8,128)(2,1)S(1)}, bf16[128,896]{1,0:T(8,128)(2,1)S(1)}, u32[]{:S(2)}, u32[]{:S(2)}) %collective-permute-start.5) | collective-permute-done | bytes 229408 | tf_op jit(solution)/shard_map/ppermute | solution.py:32
  75.4 6.6 %collective-permute-done.7.refs_3_ = bf16[128,896]{1,0:T(8,128)(2,1)S(1)} collective-permute-done((bf16[128,896]{1,0:T(8,128)(2,1)S(1)}, bf16[128,896]{1,0:T(8,128)(2,1)S(1)}, u32[]{:S(2)}, u32[]{:S(2)}) %collective-permute-start.7) | collective-permute-done | bytes 229408 | tf_op jit(solution)/shard_map/ppermute | solution.py:32
  82.0 4.8 %collective-permute-done.8.refs_4_ = bf16[128,896]{1,0:T(8,128)(2,1)S(1)} collective-permute-done((bf16[128,896]{1,0:T(8,128)(2,1)S(1)}, bf16[128,896]{1,0:T(8,128)(2,1)S(1)}, u32[]{:S(2)}, u32[]{:S(2)}) %collective-permute-start.8) | collective-permute-done | bytes 229408 | tf_op jit(solution)/shard_map/ppermute | solution.py:32
  86.8 2.4 %shard_map.88 = bf16[8,8,24,896]{3,2,1,0:T(8,128)(2,1)} custom-call(s32[1]{0:T(128)} %bitcast.level_ref, bf16[8,192,128]{2,1,0:T(8,128)(2,1)S(1)} %fusion.1.hot_ref, bf16[128,896]{1,0:T(8,128)(2,1)S(1)} %collective-permute-done.4.refs_0_, bf16[128,896]{1,0:T(8,128)(2,1)S(1)} %collective-permute-done.5.refs_1_, ...), custom_call_target="tpu_custom_call" | custom-call | tf_op jit(solution)/shard_map/pallas_call | solution.py:242
  89.2 6.1 %all-to-all-start.1 = ((bf16[8,8,24,896]{3,2,1,0:T(8,128)(2,1)}), bf16[8,8,24,896]{3,2,1,0:T(8,128)(2,1)}, u32[]{:S(2)}, u32[]{:S(2)}) async-start(bf16[8,8,24,896]{3,2,1,0:T(8,128)(2,1)} %shard_map.88), calls=%async_computation.1 | async-start | bytes 5505024 | tf_op jit(solution)/shard_map/all_to_all | solution.py:304
  95.3 3.1 %maximum_select_fusion = bf16[2,448,1024]{2,1,0:T(8,128)(2,1)} fusion(bf16[1,448,1024]{2,1,0:T(8,128)(2,1)} %bitcast.6, bf16[1,448,1024]{2,1,0:T(8,128)(2,1)S(1)} %copy-done.8, pred[]{:T(512)S(6)} %eq.27), kind=kLoop, calls=%fused_computation | loop fusion | flops 2752512 | bytes 3670017 | tf_op jit(solution)/shard_map/jit(_where)/select_n | solution.py:298
  98.5 3.1 %copy.15 = bf16[896,1024]{0,1:T(8,128)(2,1)S(1)} copy(bf16[896,1024]{1,0:T(8,128)(2,1)} %bitcast.42) | data formatting | bytes 3670016 | tf_op jit(solution)/shard_map/jit(_where)/select_n | solution.py:298
  101.5 0.1 collective-permute-start.9
  101.6 0.1 select_n.79.own_scales
  101.7 0.5 collective-permute-start.10
  102.2 23.6 %all-to-all-done.1 = bf16[8,8,24,896]{3,2,1,0:T(8,128)(2,1)} async-done(((bf16[8,8,24,896]{3,2,1,0:T(8,128)(2,1)}), bf16[8,8,24,896]{3,2,1,0:T(8,128)(2,1)}, u32[]{:S(2)}, u32[]{:S(2)}) %all-to-all-start.1) | async-done | bytes 2752544 | tf_op jit(solution)/shard_map/all_to_all | solution.py:304
  125.9 3.6 %copy.16 = bf16[8,8,24,896]{3,2,1,0:T(8,128)(2,1)} copy(bf16[8,8,24,896]{3,2,0,1:T(8,128)(2,1)} %bitcast.10) | data formatting | bytes 5505024 | tf_op jit(solution)/shard_map/transpose | solution.py:305
  129.5 4.6 %all-gather.2.cloned.1.call-done = bf16[1536,2048]{1,0:T(8,128)(2,1)} async-done(((bf16[192,2048]{1,0:T(8,128)(2,1)}), bf16[1536,2048]{1,0:T(8,128)(2,1)}) %all-gather.2.cloned.1.call-update) | async-done | bytes 6291472 | tf_op jit(solution)/shard_map/all_gather | solution.py:288
  134.1 0.5 collective-permute-start.12
  134.6 6.3 %shard_map.89 = (bf16[8,3,24,896]{3,2,1,0:T(8,128)(2,1)}, s32[5]{0:T(128)S(1)}) custom-call(s32[3]{0:T(128)S(1)} %and_select_fusion.1.place_ref.next_ref, s32[1]{0:T(128)} %bitcast.1.core_ref, s32[5]{0:T(128)S(1)} %and_select_fusion.next_ref, bf16[1024,896]{1,0:T(8,128)(2,1)S(1)} %bitcast.24, bf16[1024,896]{1,0:T(8,128)(2,1)} %collective-permute-done.9.mate_ref, ...), custom_call_target="tpu_custom_call" | custom-call | tf_op jit(solution)/shard_map/pallas_call | solution.py:123
  140.9 6.1 %all-to-all-start.2 = ((bf16[8,3,24,896]{3,2,1,0:T(8,128)(2,1)}), bf16[8,3,24,896]{3,2,1,0:T(8,128)(2,1)S(1)}, u32[]{:S(2)}, u32[]{:S(2)}) async-start(bf16[8,3,24,896]{3,2,1,0:T(8,128)(2,1)} %get-tuple-element.75), calls=%async_computation.2 | async-start | bytes 2064384 | tf_op jit(solution)/shard_map/all_to_all | solution.py:328
  147.0 8.6 %shard_map.90 = (bf16[8,5,24,896]{3,2,1,0:T(8,128)(2,1)}, s32[3]{0:T(128)}) custom-call(s32[5]{0:T(128)S(1)} %get-tuple-element.76.place_ref, s32[1]{0:T(128)} %bitcast.1.core_ref, s32[3]{0:T(128)S(1)} %and_select_fusion.1.place_ref.next_ref, bf16[1024,896]{1,0:T(8,128)(2,1)S(1)} %bitcast.25, bf16[1024,896]{1,0:T(8,128)(2,1)} %collective-permute-done.9.mate_ref, ...), custom_call_target="tpu_custom_call" | custom-call | tf_op jit(solution)/shard_map/pallas_call | solution.py:123
  155.6 5.6 %all-to-all-done.2.back_ref = bf16[8,3,24,896]{3,2,1,0:T(8,128)(2,1)S(1)} async-done(((bf16[8,3,24,896]{3,2,1,0:T(8,128)(2,1)}), bf16[8,3,24,896]{3,2,1,0:T(8,128)(2,1)S(1)}, u32[]{:S(2)}, u32[]{:S(2)}) %all-to-all-start.2) | async-done | bytes 1032224 | tf_op jit(solution)/shard_map/all_to_all | solution.py:328
  161.2 1.0 copy-done.2
  162.2 6.0 %all-to-all-start.3 = ((bf16[8,5,24,896]{3,2,1,0:T(8,128)(2,1)}), bf16[8,5,24,896]{3,2,1,0:T(8,128)(2,1)}, u32[]{:S(2)}, u32[]{:S(2)}) async-start(bf16[8,5,24,896]{3,2,1,0:T(8,128)(2,1)} %get-tuple-element.77), calls=%async_computation.3 | async-start | bytes 3440640 | tf_op jit(solution)/shard_map/all_to_all | solution.py:333
  168.2 0.1 add_select_fusion
  168.3 0.3 fusion.2
  168.6 1.3 copy-done.3
  169.9 1.1 shard_map.91
  171.0 4.1 %collective-permute-start.14 = (bf16[128,896]{1,0:T(8,128)(2,1)}, bf16[128,896]{1,0:T(8,128)(2,1)S(1)}, u32[]{:S(2)}, u32[]{:S(2)}) collective-permute-start(bf16[128,896]{1,0:T(8,128)(2,1)} %get-tuple-element.79), channel_id=1, source_target_pairs={{0,4},{1,5},{2,6},{3,7},{4,0},{5,1},{6,2},{7,3},{8,12},{9,13},{10,... | collective-permute-start | bytes 688136 | tf_op jit(solution)/shard_map/ppermute | solution.py:32
  175.1 1.4 collective-permute-start.15
  176.5 3.6 %collective-permute-start.16 = (bf16[128,896]{1,0:T(8,128)(2,1)}, bf16[128,896]{1,0:T(8,128)(2,1)S(1)}, u32[]{:S(2)}, u32[]{:S(2)}) collective-permute-start(bf16[128,896]{1,0:T(8,128)(2,1)} %get-tuple-element.81), channel_id=1, source_target_pairs={{0,5},{1,6},{2,7},{3,0},{4,1},{5,2},{6,3},{7,4},{8,13},{9,14},{10,... | collective-permute-start | bytes 688136 | tf_op jit(solution)/shard_map/ppermute | solution.py:32
  180.1 11.7 %shard_map.92 = f32[896,1024]{1,0:T(8,128)} custom-call(s32[1]{0:T(128)} %bitcast.1.core_ref, bf16[8,192,2048]{2,1,0:T(8,128)(2,1)} %bitcast.39, bf16[8,192,2048]{2,1,0:T(8,128)(2,1)} %collective-permute-done.11.mate_values_ref, bf16[1536,896]{1,0:T(8,128)(2,1)S(1)} %bitcast.27, bf16[1536,896]{1,0:T(8,128)(2,1)} %collective-permute-done.12.mate_ref), custom_call_target="tpu_custom_call" | custom-call | tf_op jit(solution)/shard_map/pallas_call | solution.py:161
  191.8 2.3 abs_reduce_fusion
  194.8 2.2 collective-permute-start.13
  197.0 0.1 collective-permute-done.15.refs_2_
  197.2 3.2 %collective-permute-done.16.refs_1_ = bf16[128,896]{1,0:T(8,128)(2,1)S(1)} collective-permute-done((bf16[128,896]{1,0:T(8,128)(2,1)}, bf16[128,896]{1,0:T(8,128)(2,1)S(1)}, u32[]{:S(2)}, u32[]{:S(2)}) %collective-permute-start.16) | collective-permute-done | bytes 229408 | tf_op jit(solution)/shard_map/ppermute | solution.py:32
  200.4 2.7 %dynamic-slice_bitcast_fusion = (f32[448,1024]{1,0:T(8,128)S(1)}, f16[448,1024]{1,0:T(8,128)(2,1)S(1)}) fusion(f32[2,448,1024]{2,1,0:T(8,128)} %bitcast.41, s32[]{:T(128)S(6)} %select_n.84, f32[]{:T(128)} %bitcast.15, s32[]{:T(128)S(6)} %select_n.83), kind=kLoop, calls=%fused_computation.2 | loop fusion | flops 917504 | bytes 6422540 | tf_op jit(solution)/shard_map/jit(dynamic_index_in_dim)/squeeze | solution.py:338
  203.1 0.9 collective-permute-start.17
  204.0 2.0 shard_map.93
  206.0 2.1 collective-permute-start.18
  208.1 1.0 collective-permute-start.19
  209.1 4.7 %collective-permute-start.20 = (bf16[128,896]{1,0:T(8,128)(2,1)S(1)}, bf16[128,896]{1,0:T(8,128)(2,1)S(1)}, u32[]{:S(2)}, u32[]{:S(2)}) collective-permute-start(bf16[128,896]{1,0:T(8,128)(2,1)S(1)} %get-tuple-element.91), channel_id=1, source_target_pairs={{0,7},{1,0},{2,1},{3,2},{4,3},{5,4},{6,5},{7,6},{8,15},{9,8},{10,9... | collective-permute-start | bytes 688136 | tf_op jit(solution)/shard_map/ppermute | solution.py:32
  213.7 9.6 %collective-permute-done.17 = f16[448,1024]{1,0:T(8,128)(2,1)S(1)} collective-permute-done((f16[448,1024]{1,0:T(8,128)(2,1)S(1)}, f16[448,1024]{1,0:T(8,128)(2,1)S(1)}, u32[]{:S(2)}, u32[]{:S(2)}) %collective-permute-start.17) | collective-permute-done | bytes 917536 | tf_op jit(solution)/shard_map/ppermute | solution.py:343
  223.4 2.3 multiply_add_fusion
  225.6 1.5 collective-permute-done.21.refs_6_
  227.1 1.8 shard_map.94
  (56 shorter events, 0.9 us)
Async XLA Ops:
  7.2 0.7 copy-start
  7.2 11.3 %copy-start.4 = (bf16[128,7168]{1,0:T(8,128)(2,1)S(1)}, bf16[128,7168]{1,0:T(8,128)(2,1)}, u32[]{:S(2)}) copy-start(bf16[128,7168]{1,0:T(8,128)(2,1)} %hidden_ref.1) | copy-start | bytes 5505028
  8.1 1.0 copy-start.5
  10.9 19.1 %copy-start.9 = (f32[1,448]{1,0:T(1,128)S(1)}, f32[1,448]{1,0:T(1,128)}, u32[]{:S(2)}) copy-start(f32[1,448]{1,0:T(1,128)} %param.10) | copy-start | bytes 5380
  10.9 19.1 %all-to-all-start = ((bf16[8,24,2048]{2,1,0:T(8,128)(2,1)}), bf16[8,24,2048]{2,1,0:T(8,128)(2,1)}, u32[]{:S(2)}, u32[]{:S(2)}) async-start(bf16[8,24,2048]{2,1,0:T(8,128)(2,1)} %shard_map.86), calls=%async_computation | async-start | bytes 1572864 | tf_op jit(solution)/shard_map/all_to_all | solution.py:280
  18.4 115.6 %all-gather.2.cloned.1.call-start = ((), (), s32[]{:S(2)}) async-start(), calls=%async_computation.4 | async-start | bytes 7077888 | tf_op jit(solution)/shard_map/all_gather | solution.py:288
  18.9 11.0 %collective-permute-start = (bf16[128,896]{1,0:T(8,128)(2,1)S(1)}, bf16[128,896]{1,0:T(8,128)(2,1)S(1)}, u32[]{:S(2)}, u32[]{:S(2)}) collective-permute-start(bf16[128,896]{1,0:T(8,128)(2,1)S(1)} %get-tuple-element.48), channel_id=1, source_target_pairs={{0,1},{1,2},{2,3},{3,4},{4,5},{5,6},{6,7},{7,0},{8,9},{9,10},{10,1... | collective-permute-start | bytes 688136 | tf_op jit(solution)/shard_map/ppermute | solution.py:32
  20.9 9.0 %collective-permute-start.1 = (bf16[128,896]{1,0:T(8,128)(2,1)S(1)}, bf16[128,896]{1,0:T(8,128)(2,1)S(1)}, u32[]{:S(2)}, u32[]{:S(2)}) collective-permute-start(bf16[128,896]{1,0:T(8,128)(2,1)S(1)} %get-tuple-element.49), channel_id=1, source_target_pairs={{0,7},{1,0},{2,1},{3,2},{4,3},{5,4},{6,5},{7,6},{8,15},{9,8},{10,9... | collective-permute-start | bytes 688136 | tf_op jit(solution)/shard_map/ppermute | solution.py:32
  30.0 14.1 %collective-permute-start.3 = (f32[448]{0:T(512)S(1)}, f32[448]{0:T(512)S(1)}, u32[]{:S(2)}, u32[]{:S(2)}) collective-permute-start(f32[448]{0:T(512)S(1)} %bitcast.45), channel_id=1, source_target_pairs={{0,8},{8,0},{1,9},{9,1},{2,10},{10,2},{3,11},{11,3},{4,12},{12,4},... | collective-permute-start | bytes 5384 | tf_op jit(solution)/shard_map/ppermute | solution.py:276
  30.9 55.9 %collective-permute-start.2 = (bf16[448,1024]{1,0:T(8,128)(2,1)}, bf16[448,1024]{1,0:T(8,128)(2,1)}, u32[]{:S(2)}, u32[]{:S(2)}) collective-permute-start(bf16[448,1024]{1,0:T(8,128)(2,1)} %bitcast.44), channel_id=1, source_target_pairs={{0,8},{8,0},{1,9},{9,1},{2,10},{10,2},{3,11},{11,3},{4,12},{12,4},... | collective-permute-start | bytes 2752520 | tf_op jit(solution)/shard_map/ppermute | solution.py:276
  32.1 22.2 %collective-permute-start.4 = (bf16[128,896]{1,0:T(8,128)(2,1)S(1)}, bf16[128,896]{1,0:T(8,128)(2,1)S(1)}, u32[]{:S(2)}, u32[]{:S(2)}) collective-permute-start(bf16[128,896]{1,0:T(8,128)(2,1)S(1)} %get-tuple-element.51), channel_id=1, source_target_pairs={{0,4},{1,5},{2,6},{3,7},{4,0},{5,1},{6,2},{7,3},{8,12},{9,13},{10,... | collective-permute-start | bytes 688136 | tf_op jit(solution)/shard_map/ppermute | solution.py:32
  39.3 36.1 %collective-permute-start.5 = (bf16[128,896]{1,0:T(8,128)(2,1)S(1)}, bf16[128,896]{1,0:T(8,128)(2,1)S(1)}, u32[]{:S(2)}, u32[]{:S(2)}) collective-permute-start(bf16[128,896]{1,0:T(8,128)(2,1)S(1)} %get-tuple-element.52), channel_id=1, source_target_pairs={{0,5},{1,6},{2,7},{3,0},{4,1},{5,2},{6,3},{7,4},{8,13},{9,14},{10,... | collective-permute-start | bytes 688136 | tf_op jit(solution)/shard_map/ppermute | solution.py:32
  39.3 36.1 %collective-permute-start.6 = (bf16[128,896]{1,0:T(8,128)(2,1)S(1)}, bf16[128,896]{1,0:T(8,128)(2,1)S(1)}, u32[]{:S(2)}, u32[]{:S(2)}) collective-permute-start(bf16[128,896]{1,0:T(8,128)(2,1)S(1)} %get-tuple-element.53), channel_id=1, source_target_pairs={{0,3},{1,4},{2,5},{3,6},{4,7},{5,0},{6,1},{7,2},{8,11},{9,12},{10,... | collective-permute-start | bytes 688136 | tf_op jit(solution)/shard_map/ppermute | solution.py:32
  44.1 37.9 %collective-permute-start.7 = (bf16[128,896]{1,0:T(8,128)(2,1)S(1)}, bf16[128,896]{1,0:T(8,128)(2,1)S(1)}, u32[]{:S(2)}, u32[]{:S(2)}) collective-permute-start(bf16[128,896]{1,0:T(8,128)(2,1)S(1)} %get-tuple-element.54), channel_id=1, source_target_pairs={{0,6},{1,7},{2,0},{3,1},{4,2},{5,3},{6,4},{7,5},{8,14},{9,15},{10,... | collective-permute-start | bytes 688136 | tf_op jit(solution)/shard_map/ppermute | solution.py:32
  54.3 32.5 %collective-permute-start.8 = (bf16[128,896]{1,0:T(8,128)(2,1)S(1)}, bf16[128,896]{1,0:T(8,128)(2,1)S(1)}, u32[]{:S(2)}, u32[]{:S(2)}) collective-permute-start(bf16[128,896]{1,0:T(8,128)(2,1)S(1)} %get-tuple-element.55), channel_id=1, source_target_pairs={{0,2},{1,3},{2,4},{3,5},{4,6},{5,7},{6,0},{7,1},{8,10},{9,11},{10,... | collective-permute-start | bytes 688136 | tf_op jit(solution)/shard_map/ppermute | solution.py:32
  89.2 6.1 %copy-start.8 = (bf16[1,448,1024]{2,1,0:T(8,128)(2,1)S(1)}, bf16[1,448,1024]{2,1,0:T(8,128)(2,1)}, u32[]{:S(2)}) copy-start(bf16[1,448,1024]{2,1,0:T(8,128)(2,1)} %param.9) | copy-start | bytes 2752516
  89.2 36.7 %all-to-all-start.1 = ((bf16[8,8,24,896]{3,2,1,0:T(8,128)(2,1)}), bf16[8,8,24,896]{3,2,1,0:T(8,128)(2,1)}, u32[]{:S(2)}, u32[]{:S(2)}) async-start(bf16[8,8,24,896]{3,2,1,0:T(8,128)(2,1)} %shard_map.88), calls=%async_computation.1 | async-start | bytes 5505024 | tf_op jit(solution)/shard_map/all_to_all | solution.py:304
  101.5 27.9 %collective-permute-start.9 = (bf16[1024,896]{1,0:T(8,128)(2,1)S(1)}, bf16[1024,896]{1,0:T(8,128)(2,1)}, u32[]{:S(2)}, u32[]{:S(2)}) collective-permute-start(bf16[1024,896]{1,0:T(8,128)(2,1)S(1)} %bitcast.23), channel_id=1, source_target_pairs={{0,16},{16,0},{1,17},{17,1},{2,18},{18,2},{3,19},{19,3},{4,20},{20... | collective-permute-start | bytes 5505032 | tf_op jit(solution)/shard_map/ppermute | solution.py:302
  101.7 27.7 %collective-permute-start.10 = (f32[1,896]{1,0:T(1,128)S(1)}, f32[1,896]{1,0:T(1,128)S(1)}, u32[]{:S(2)}, u32[]{:S(2)}) collective-permute-start(f32[1,896]{1,0:T(1,128)S(1)} %select_n.79.own_scales), channel_id=1, source_target_pairs={{0,16},{16,0},{1,17},{17,1},{2,18},{18,2},{3,19},{19,3},{4,20},{20... | collective-permute-start | bytes 10760 | tf_op jit(solution)/shard_map/ppermute | solution.py:302
  125.9 8.7 %copy-start.11 = (s32[3]{0:T(128)S(1)}, s32[3]{0:T(128)}, u32[]{:S(2)}) copy-start(s32[3]{0:T(128)} %constant.80.clone) | copy-start | bytes 40
  125.9 8.7 %copy-start.10 = (s32[5]{0:T(128)S(1)}, s32[5]{0:T(128)}, u32[]{:S(2)}) copy-start(s32[5]{0:T(128)} %constant.81.clone) | copy-start | bytes 64
  134.0 46.1 %collective-permute-start.11 = (bf16[8,192,2048]{2,1,0:T(8,128)(2,1)}, bf16[8,192,2048]{2,1,0:T(8,128)(2,1)}, u32[]{:S(2)}, u32[]{:S(2)}) collective-permute-start(bf16[8,192,2048]{2,1,0:T(8,128)(2,1)} %bitcast.30), channel_id=1, source_target_pairs={{0,16},{16,0},{1,17},{17,1},{2,18},{18,2},{3,19},{19,3},{4,20},{20... | collective-permute-start | bytes 18874376 | tf_op jit(solution)/shard_map/ppermute | solution.py:327
  134.1 46.0 %collective-permute-start.12 = (bf16[1536,896]{1,0:T(8,128)(2,1)}, bf16[1536,896]{1,0:T(8,128)(2,1)}, u32[]{:S(2)}, u32[]{:S(2)}) collective-permute-start(bf16[1536,896]{1,0:T(8,128)(2,1)} %bitcast.26), channel_id=1, source_target_pairs={{0,16},{16,0},{1,17},{17,1},{2,18},{18,2},{3,19},{19,3},{4,20},{20... | collective-permute-start | bytes 8257544 | tf_op jit(solution)/shard_map/ppermute | solution.py:306
  140.9 20.3 %all-to-all-start.2 = ((bf16[8,3,24,896]{3,2,1,0:T(8,128)(2,1)}), bf16[8,3,24,896]{3,2,1,0:T(8,128)(2,1)S(1)}, u32[]{:S(2)}, u32[]{:S(2)}) async-start(bf16[8,3,24,896]{3,2,1,0:T(8,128)(2,1)} %get-tuple-element.75), calls=%async_computation.2 | async-start | bytes 2064384 | tf_op jit(solution)/shard_map/all_to_all | solution.py:328
  161.2 1.0 copy-start.2
  162.2 17.9 %copy-start.1 = (bf16[8,8,24,896]{3,2,1,0:T(8,128)(2,1)S(1)}, bf16[8,8,24,896]{3,2,1,0:T(8,128)(2,1)}, u32[]{:S(2)}) copy-start(bf16[8,8,24,896]{3,2,1,0:T(8,128)(2,1)} %copy.16) | copy-start | bytes 8257540
  162.2 38.2 %all-to-all-start.3 = ((bf16[8,5,24,896]{3,2,1,0:T(8,128)(2,1)}), bf16[8,5,24,896]{3,2,1,0:T(8,128)(2,1)}, u32[]{:S(2)}, u32[]{:S(2)}) async-start(bf16[8,5,24,896]{3,2,1,0:T(8,128)(2,1)} %get-tuple-element.77), calls=%async_computation.3 | async-start | bytes 3440640 | tf_op jit(solution)/shard_map/all_to_all | solution.py:333
  168.5 8.0 %copy-start.6 = (bf16[8,8,24,128]{3,2,1,0:T(8,128)(2,1)}, bf16[8,8,24,128]{3,2,1,0:T(8,128)(2,1)S(1)}, u32[]{:S(2)}) copy-start(bf16[8,8,24,128]{3,2,1,0:T(8,128)(2,1)S(1)} %fusion.2) | copy-start | bytes 1179652
  168.6 1.3 copy-start.3
  171.0 26.0 %collective-permute-start.14 = (bf16[128,896]{1,0:T(8,128)(2,1)}, bf16[128,896]{1,0:T(8,128)(2,1)S(1)}, u32[]{:S(2)}, u32[]{:S(2)}) collective-permute-start(bf16[128,896]{1,0:T(8,128)(2,1)} %get-tuple-element.79), channel_id=1, source_target_pairs={{0,4},{1,5},{2,6},{3,7},{4,0},{5,1},{6,2},{7,3},{8,12},{9,13},{10,... | collective-permute-start | bytes 688136 | tf_op jit(solution)/shard_map/ppermute | solution.py:32
  175.1 22.1 %collective-permute-start.15 = (bf16[128,896]{1,0:T(8,128)(2,1)}, bf16[128,896]{1,0:T(8,128)(2,1)S(1)}, u32[]{:S(2)}, u32[]{:S(2)}) collective-permute-start(bf16[128,896]{1,0:T(8,128)(2,1)} %get-tuple-element.80), channel_id=1, source_target_pairs={{0,3},{1,4},{2,5},{3,6},{4,7},{5,0},{6,1},{7,2},{8,11},{9,12},{10,... | collective-permute-start | bytes 688136 | tf_op jit(solution)/shard_map/ppermute | solution.py:32
  176.5 23.9 %collective-permute-start.16 = (bf16[128,896]{1,0:T(8,128)(2,1)}, bf16[128,896]{1,0:T(8,128)(2,1)S(1)}, u32[]{:S(2)}, u32[]{:S(2)}) collective-permute-start(bf16[128,896]{1,0:T(8,128)(2,1)} %get-tuple-element.81), channel_id=1, source_target_pairs={{0,5},{1,6},{2,7},{3,0},{4,1},{5,2},{6,3},{7,4},{8,13},{9,14},{10,... | collective-permute-start | bytes 688136 | tf_op jit(solution)/shard_map/ppermute | solution.py:32
  194.8 8.3 %collective-permute-start.13 = (f32[1]{0:T(128)}, f32[1]{0:T(128)}, u32[]{:S(2)}, u32[]{:S(2)}) collective-permute-start(f32[1]{0:T(128)} %bitcast.14), channel_id=1, source_target_pairs={{0,8},{8,0},{1,9},{9,1},{2,10},{10,2},{3,11},{11,3},{4,12},{12,4},... | collective-permute-start | bytes 20 | tf_op jit(solution)/shard_map/ppermute | solution.py:341
  200.4 3.6 %copy-start.7 = (bf16[8,8,24,128]{3,2,1,0:T(8,128)(2,1)S(1)}, bf16[8,8,24,128]{3,2,1,0:T(8,128)(2,1)}, u32[]{:S(2)}) copy-start(bf16[8,8,24,128]{3,2,1,0:T(8,128)(2,1)} %copy-done.6) | copy-start | bytes 1179652
  203.1 20.3 %collective-permute-start.17 = (f16[448,1024]{1,0:T(8,128)(2,1)S(1)}, f16[448,1024]{1,0:T(8,128)(2,1)S(1)}, u32[]{:S(2)}, u32[]{:S(2)}) collective-permute-start(f16[448,1024]{1,0:T(8,128)(2,1)S(1)} %get-tuple-element.86), channel_id=1, source_target_pairs={{0,8},{8,0},{1,9},{9,1},{2,10},{10,2},{3,11},{11,3},{4,12},{12,4},... | collective-permute-start | bytes 2752520 | tf_op jit(solution)/shard_map/ppermute | solution.py:343
  206.0 19.6 %collective-permute-start.18 = (bf16[128,896]{1,0:T(8,128)(2,1)S(1)}, bf16[128,896]{1,0:T(8,128)(2,1)S(1)}, u32[]{:S(2)}, u32[]{:S(2)}) collective-permute-start(bf16[128,896]{1,0:T(8,128)(2,1)S(1)} %get-tuple-element.89), channel_id=1, source_target_pairs={{0,6},{1,7},{2,0},{3,1},{4,2},{5,3},{6,4},{7,5},{8,14},{9,15},{10,... | collective-permute-start | bytes 688136 | tf_op jit(solution)/shard_map/ppermute | solution.py:32
  208.1 17.6 %collective-permute-start.19 = (bf16[128,896]{1,0:T(8,128)(2,1)S(1)}, bf16[128,896]{1,0:T(8,128)(2,1)S(1)}, u32[]{:S(2)}, u32[]{:S(2)}) collective-permute-start(bf16[128,896]{1,0:T(8,128)(2,1)S(1)} %get-tuple-element.90), channel_id=1, source_target_pairs={{0,2},{1,3},{2,4},{3,5},{4,6},{5,7},{6,0},{7,1},{8,10},{9,11},{10,... | collective-permute-start | bytes 688136 | tf_op jit(solution)/shard_map/ppermute | solution.py:32
  209.1 16.6 %collective-permute-start.20 = (bf16[128,896]{1,0:T(8,128)(2,1)S(1)}, bf16[128,896]{1,0:T(8,128)(2,1)S(1)}, u32[]{:S(2)}, u32[]{:S(2)}) collective-permute-start(bf16[128,896]{1,0:T(8,128)(2,1)S(1)} %get-tuple-element.91), channel_id=1, source_target_pairs={{0,7},{1,0},{2,1},{3,2},{4,3},{5,4},{6,5},{7,6},{8,15},{9,8},{10,9... | collective-permute-start | bytes 688136 | tf_op jit(solution)/shard_map/ppermute | solution.py:32
  213.7 13.4 %collective-permute-start.21 = (bf16[128,896]{1,0:T(8,128)(2,1)S(1)}, bf16[128,896]{1,0:T(8,128)(2,1)S(1)}, u32[]{:S(2)}, u32[]{:S(2)}) collective-permute-start(bf16[128,896]{1,0:T(8,128)(2,1)S(1)} %get-tuple-element.92), channel_id=1, source_target_pairs={{0,1},{1,2},{2,3},{3,4},{4,5},{5,6},{6,7},{7,0},{8,9},{9,10},{10,1... | collective-permute-start | bytes 688136 | tf_op jit(solution)/shard_map/ppermute | solution.py:32
Sparse Core Ops, SparseCore 0:
  30.1 103.8 all-gather.1
where the time goes:
time: 237 us; the launch traced here: 236 us
  waiting for transfers between devices  87.1 us (37%)
  starting transfers between devices  74.6 us (31%)
  Pallas kernels  36.1 us (15%)
  between operations  15 us (6%)
  local copies, waits for them, and re-layouts  11.8 us (5%)
  other arithmetic  11.1 us (5%)
    ppermute x14, waiting for transfers between devices, along_z(): lax.ppermute(value, 'z', [(i, (i + by) % depth) for i in range(depth)])  43.5 us
    ppermute x14, starting transfers between devices, along_z(): lax.ppermute(value, 'z', [(i, (i + by) % depth) for i in range(depth)])  42.5 us
    all_to_all x1, waiting for transfers between devices, shards(): own_hidden = lax.all_to_all(hidden_slots, PLACES, 0, 0)  23.6 us
    pallas_call x2, Pallas kernels, join_rows(): pl.pallas_call(join_rows_kernel, out_shape=[pltpu.HBM(shape, jnp.bfloat16...  14.9 us
    pallas_call x1, Pallas kernels, weight_sums(): pl.pallas_call(weight_kernel, out_shape=pltpu.HBM((wide, half), jnp.float...  11.7 us
    ppermute x1, waiting for transfers between devices, shards(): gone = lax.ppermute(gone, 'xl', SWAP)  9.63 us
    all_to_all x1, starting transfers between devices, shards(): arrived = lax.all_to_all(packed, PLACES, 0, 0).reshape(places * slots, cols)  7.57 us
    all_to_all x1, starting transfers between devices, shards(): own_hidden = lax.all_to_all(hidden_slots, PLACES, 0, 0)  6.14 us
  transfers between devices with their start and end apart: 27, of which 13 were waited for; matrix products, arithmetic and copies ran while one was open for 8% of the time, Pallas kernels for 14%

commit v1 on v0

--- a/solution.py
+++ b/solution.py
@@ -92,19 +92,26 @@
 
 
 def join_rows_kernel(place_ref, core_ref, next_ref, own_ref, mate_ref, own_scales, mate_scales, *refs):
-    rows_refs, out_ref, passed_ref = refs[:-2], refs[-2], refs[-1]
+    rows_refs, out_ref, passed_ref, held = refs[:-3], refs[-3], refs[-2], refs[-1]
     for i in range(next_ref.shape[0]):
         passed_ref[i] = next_ref[i]
-    half = own_ref.shape[0]
-    pairs = [halves_of(ref, core_ref[0], half) for ref in rows_refs]
-    own = jnp.concatenate([pair[0][0] for pair in pairs])
-    mate = jnp.concatenate([pair[1][0] for pair in pairs])
-    total = own_scales[...] * jnp.dot(own, own_ref[...], preferred_element_type=jnp.float32)
-    total += mate_scales[...] * jnp.dot(mate, mate_ref[...], preferred_element_type=jnp.float32)
-    places, steps, slots, wide = out_ref.shape
-    total = total.reshape(steps, places, slots, wide).astype(out_ref.dtype)
-    for step in range(steps):
-        out_ref[:, step] = total[step]
+    values = jnp.concatenate([ref[0] for ref in rows_refs])
+
+    @pl.when(pl.program_id(0) == 0)
+    def _():
+        held[...] = own_scales[...] * jnp.dot(
+            values, own_ref[...], preferred_element_type=jnp.float32
+        )
+
+    @pl.when(pl.program_id(0) == 1)
+    def _():
+        total = held[...] + mate_scales[...] * jnp.dot(
+            values, mate_ref[...], preferred_element_type=jnp.float32
+        )
+        places, steps, slots, wide = out_ref.shape
+        total = total.reshape(steps, places, slots, wide).astype(out_ref.dtype)
+        for step in range(steps):
+            out_ref[:, step] = total[step]
 
 
 def join_rows(where, core, then, values, codes, scales, places):
@@ -113,7 +120,7 @@
     half, wide = codes[0].shape
 
     def rows_spec(j):
-        return pl.BlockSpec((1, rows, cols), lambda i, w, c: (w[j], 0, 0))
+        return pl.BlockSpec((1, rows, half), lambda i, w, c: (w[j], 0, c[0] ^ i))
 
     def whole(*shape):
         return pl.BlockSpec(shape, lambda i, w, c: (0,) * len(shape))
@@ -125,10 +132,11 @@
         out_shape=[pltpu.HBM(shape, jnp.bfloat16), jax.ShapeDtypeStruct(then.shape, then.dtype)],
         grid_spec=pltpu.PrefetchScalarGridSpec(
             num_scalar_prefetch=2,
-            grid=(1,),
+            grid=(2,),
             in_specs=[words] + [whole(half, wide)] * 2 + [whole(1, wide)] * 2
             + [rows_spec(j) for j in range(steps)],
             out_specs=[whole(*shape), words],
+            scratch_shapes=[pltpu.VMEM((steps * rows, wide), jnp.float32)],
         ),
         compiler_params=pltpu.CompilerParams(vmem_limit_bytes=40 << 20),
     )(where, core, then, *codes, *scales, *[values] * steps)
@@ -326,6 +334,7 @@
     close_joined, _ = join(close_at, far_at)
     mate_values = lax.ppermute(gathered, "c", SWAP)
     far_raw = after(lax.all_to_all(far_joined, PLACES, 0, 0), close_joined)
+    far_raw = pltpu.with_memory_space_constraint(far_raw, pltpu.HBM)
     far_back = unpack(near_hot[:cut], far_raw)
     send_home(order[:cut], far_back)
     own_hidden, mate_hidden = after((own_hidden, mate_hidden), *far_back)

time: 237 us -> 237 us (level)
  transfers between devices with their start and end apart: 27 -> 27, of which waited for: 13 -> 13; matrix products, arithmetic and copies ran while one was open for 8% -> 8% of each run, Pallas kernels for 14% -> 15%
where the time goes in v1:
time: 237 us; the launch traced here: 236 us
  waiting for transfers between devices  86.6 us (37%)
  starting transfers between devices  74.6 us (31%)
  Pallas kernels  38.1 us (16%)
  between operations  15 us (6%)
  other arithmetic  11.1 us (5%)
  local copies, waits for them, and re-layouts  10.5 us (4%)
    ppermute x14, waiting for transfers between devices, along_z(): lax.ppermute(value, 'z', [(i, (i + by) % depth) for i in range(depth)])  43.5 us
    ppermute x14, starting transfers between devices, along_z(): lax.ppermute(value, 'z', [(i, (i + by) % depth) for i in range(depth)])  41.1 us
    all_to_all x1, waiting for transfers between devices, shards(): own_hidden = lax.all_to_all(hidden_slots, PLACES, 0, 0)  23.5 us
    pallas_call x2, Pallas kernels, join_rows(): pl.pallas_call(join_rows_kernel, out_shape=[pltpu.HBM(shape, jnp.bfloat16...  15.5 us
    pallas_call x1, Pallas kernels, weight_sums(): pl.pallas_call(weight_kernel, out_shape=pltpu.HBM((wide, half), jnp.float...  11.7 us
    ppermute x1, waiting for transfers between devices, shards(): gone = lax.ppermute(gone, 'xl', SWAP)  9.62 us
    all_to_all x1, starting transfers between devices, shards(): arrived = lax.all_to_all(packed, PLACES, 0, 0).reshape(places * slots, cols)  7.57 us
    all_to_all x1, starting transfers between devices, shards(): own_hidden = lax.all_to_all(hidden_slots, PLACES, 0, 0)  6.14 us
  transfers between devices with their start and end apart: 27, of which 13 were waited for; matrix products, arithmetic and copies ran while one was open for 8% of the time, Pallas kernels for 15%

profile of v1, /device:TPU:6, one launch (start us, length us, event | category | flops | bytes accessed | tf_op | source)
XLA Modules:
  0.0 235.9 jit_solution(14350698422464477311)
XLA Ops:
  7.2 0.7 copy-done
  7.9 0.2 dynamic-slice_reduce_fusion.counts_ref
  8.1 1.0 copy-done.3
  9.1 1.8 shard_map.86
  10.9 7.6 %all-to-all-start = ((bf16[8,24,2048]{2,1,0:T(8,128)(2,1)}), bf16[8,24,2048]{2,1,0:T(8,128)(2,1)}, u32[]{:S(2)}, u32[]{:S(2)}) async-start(bf16[8,24,2048]{2,1,0:T(8,128)(2,1)} %shard_map.86), calls=%async_computation | async-start | bytes 1572864 | tf_op jit(solution)/shard_map/all_to_all | solution.py:288
  18.4 0.5 shard_map.87
  18.9 2.0 collective-permute-start
  20.9 4.0 %collective-permute-start.1 = (bf16[128,896]{1,0:T(8,128)(2,1)S(1)}, bf16[128,896]{1,0:T(8,128)(2,1)S(1)}, u32[]{:S(2)}, u32[]{:S(2)}) collective-permute-start(bf16[128,896]{1,0:T(8,128)(2,1)S(1)} %get-tuple-element.49), channel_id=1, source_target_pairs={{0,7},{1,0},{2,1},{3,2},{4,3},{5,4},{6,5},{7,6},{8,15},{9,8},{10,9... | collective-permute-start | bytes 688136 | tf_op jit(solution)/shard_map/ppermute | solution.py:32
  25.0 5.0 %collective-permute-done.refs_6_ = bf16[128,896]{1,0:T(8,128)(2,1)S(1)} collective-permute-done((bf16[128,896]{1,0:T(8,128)(2,1)S(1)}, bf16[128,896]{1,0:T(8,128)(2,1)S(1)}, u32[]{:S(2)}, u32[]{:S(2)}) %collective-permute-start) | collective-permute-done | bytes 229408 | tf_op jit(solution)/shard_map/ppermute | solution.py:32
  30.0 0.9 collective-permute-start.3
  30.9 1.2 collective-permute-start.2
  32.1 7.2 %collective-permute-start.4 = (bf16[128,896]{1,0:T(8,128)(2,1)S(1)}, bf16[128,896]{1,0:T(8,128)(2,1)S(1)}, u32[]{:S(2)}, u32[]{:S(2)}) collective-permute-start(bf16[128,896]{1,0:T(8,128)(2,1)S(1)} %get-tuple-element.51), channel_id=1, source_target_pairs={{0,4},{1,5},{2,6},{3,7},{4,0},{5,1},{6,2},{7,3},{8,12},{9,13},{10,... | collective-permute-start | bytes 688136 | tf_op jit(solution)/shard_map/ppermute | solution.py:32
  39.3 3.8 %collective-permute-start.6 = (bf16[128,896]{1,0:T(8,128)(2,1)S(1)}, bf16[128,896]{1,0:T(8,128)(2,1)S(1)}, u32[]{:S(2)}, u32[]{:S(2)}) collective-permute-start(bf16[128,896]{1,0:T(8,128)(2,1)S(1)} %get-tuple-element.53), channel_id=1, source_target_pairs={{0,3},{1,4},{2,5},{3,6},{4,7},{5,0},{6,1},{7,2},{8,11},{9,12},{10,... | collective-permute-start | bytes 688136 | tf_op jit(solution)/shard_map/ppermute | solution.py:32
  43.2 0.1 pad_add_fusion
  43.4 0.1 fusion.5
  43.4 0.1 stack.23
  43.6 0.1 lt.66
  43.9 0.1 lt.71
  43.9 0.1 add.89
  44.1 0.9 collective-permute-start.7
  45.1 9.3 %collective-permute-done.4.refs_0_ = bf16[128,896]{1,0:T(8,128)(2,1)S(1)} collective-permute-done((bf16[128,896]{1,0:T(8,128)(2,1)S(1)}, bf16[128,896]{1,0:T(8,128)(2,1)S(1)}, u32[]{:S(2)}, u32[]{:S(2)}) %collective-permute-start.4) | collective-permute-done | bytes 229408 | tf_op jit(solution)/shard_map/ppermute | solution.py:32
  54.3 7.7 %collective-permute-start.8 = (bf16[128,896]{1,0:T(8,128)(2,1)S(1)}, bf16[128,896]{1,0:T(8,128)(2,1)S(1)}, u32[]{:S(2)}, u32[]{:S(2)}) collective-permute-start(bf16[128,896]{1,0:T(8,128)(2,1)S(1)} %get-tuple-element.55), channel_id=1, source_target_pairs={{0,2},{1,3},{2,4},{3,5},{4,6},{5,7},{6,0},{7,1},{8,10},{9,11},{10,... | collective-permute-start | bytes 688136 | tf_op jit(solution)/shard_map/ppermute | solution.py:32
  62.1 0.3 fusion.1.hot_ref
  62.4 13.1 %collective-permute-done.5.refs_1_ = bf16[128,896]{1,0:T(8,128)(2,1)S(1)} collective-permute-done((bf16[128,896]{1,0:T(8,128)(2,1)S(1)}, bf16[128,896]{1,0:T(8,128)(2,1)S(1)}, u32[]{:S(2)}, u32[]{:S(2)}) %collective-permute-start.5) | collective-permute-done | bytes 229408 | tf_op jit(solution)/shard_map/ppermute | solution.py:32
  75.4 6.6 %collective-permute-done.7.refs_3_ = bf16[128,896]{1,0:T(8,128)(2,1)S(1)} collective-permute-done((bf16[128,896]{1,0:T(8,128)(2,1)S(1)}, bf16[128,896]{1,0:T(8,128)(2,1)S(1)}, u32[]{:S(2)}, u32[]{:S(2)}) %collective-permute-start.7) | collective-permute-done | bytes 229408 | tf_op jit(solution)/shard_map/ppermute | solution.py:32
  82.0 4.8 %collective-permute-done.8.refs_4_ = bf16[128,896]{1,0:T(8,128)(2,1)S(1)} collective-permute-done((bf16[128,896]{1,0:T(8,128)(2,1)S(1)}, bf16[128,896]{1,0:T(8,128)(2,1)S(1)}, u32[]{:S(2)}, u32[]{:S(2)}) %collective-permute-start.8) | collective-permute-done | bytes 229408 | tf_op jit(solution)/shard_map/ppermute | solution.py:32
  86.8 2.4 %shard_map.88 = bf16[8,8,24,896]{3,2,1,0:T(8,128)(2,1)} custom-call(s32[1]{0:T(128)} %bitcast.level_ref, bf16[8,192,128]{2,1,0:T(8,128)(2,1)S(1)} %fusion.1.hot_ref, bf16[128,896]{1,0:T(8,128)(2,1)S(1)} %collective-permute-done.4.refs_0_, bf16[128,896]{1,0:T(8,128)(2,1)S(1)} %collective-permute-done.5.refs_1_, ...), custom_call_target="tpu_custom_call" | custom-call | tf_op jit(solution)/shard_map/pallas_call | solution.py:250
  89.2 6.1 %all-to-all-start.1 = ((bf16[8,8,24,896]{3,2,1,0:T(8,128)(2,1)}), bf16[8,8,24,896]{3,2,1,0:T(8,128)(2,1)}, u32[]{:S(2)}, u32[]{:S(2)}) async-start(bf16[8,8,24,896]{3,2,1,0:T(8,128)(2,1)} %shard_map.88), calls=%async_computation.1 | async-start | bytes 5505024 | tf_op jit(solution)/shard_map/all_to_all | solution.py:312
  95.3 3.2 %maximum_select_fusion = bf16[2,448,1024]{2,1,0:T(8,128)(2,1)} fusion(bf16[1,448,1024]{2,1,0:T(8,128)(2,1)} %bitcast.6, bf16[1,448,1024]{2,1,0:T(8,128)(2,1)S(1)} %copy-done.7, pred[]{:T(512)S(6)} %eq.27), kind=kLoop, calls=%fused_computation | loop fusion | flops 2752512 | bytes 3670017 | tf_op jit(solution)/shard_map/jit(_where)/select_n | solution.py:306
  98.5 3.1 %copy.15 = bf16[896,1024]{0,1:T(8,128)(2,1)S(1)} copy(bf16[896,1024]{1,0:T(8,128)(2,1)} %bitcast.42) | data formatting | bytes 3670016 | tf_op jit(solution)/shard_map/jit(_where)/select_n | solution.py:306
  101.6 0.1 collective-permute-start.9
  101.7 0.1 select_n.79.own_scales
  101.8 0.5 collective-permute-start.10
  102.3 23.5 %all-to-all-done.1 = bf16[8,8,24,896]{3,2,1,0:T(8,128)(2,1)} async-done(((bf16[8,8,24,896]{3,2,1,0:T(8,128)(2,1)}), bf16[8,8,24,896]{3,2,1,0:T(8,128)(2,1)}, u32[]{:S(2)}, u32[]{:S(2)}) %all-to-all-start.1) | async-done | bytes 2752544 | tf_op jit(solution)/shard_map/all_to_all | solution.py:312
  125.9 3.6 %copy.16 = bf16[8,8,24,896]{3,2,1,0:T(8,128)(2,1)} copy(bf16[8,8,24,896]{3,2,0,1:T(8,128)(2,1)} %bitcast.10) | data formatting | bytes 5505024 | tf_op jit(solution)/shard_map/transpose | solution.py:313
  129.5 4.6 %all-gather.2.cloned.1.call-done = bf16[1536,2048]{1,0:T(8,128)(2,1)} async-done(((bf16[192,2048]{1,0:T(8,128)(2,1)}), bf16[1536,2048]{1,0:T(8,128)(2,1)}) %all-gather.2.cloned.1.call-update) | async-done | bytes 6291472 | tf_op jit(solution)/shard_map/all_gather | solution.py:296
  134.1 0.5 collective-permute-start.12
  134.6 6.6 %shard_map.89 = (bf16[8,3,24,896]{3,2,1,0:T(8,128)(2,1)}, s32[5]{0:T(128)S(1)}) custom-call(s32[3]{0:T(128)S(1)} %and_select_fusion.1.place_ref.next_ref, s32[1]{0:T(128)} %bitcast.1.core_ref, s32[5]{0:T(128)S(1)} %and_select_fusion.next_ref, bf16[1024,896]{1,0:T(8,128)(2,1)S(1)} %bitcast.24, bf16[1024,896]{1,0:T(8,128)(2,1)} %collective-permute-done.9.mate_ref, ...), custom_call_target="tpu_custom_call" | custom-call | tf_op jit(solution)/shard_map/pallas_call | solution.py:130
  141.2 6.1 %all-to-all-start.2 = ((bf16[8,3,24,896]{3,2,1,0:T(8,128)(2,1)}), bf16[8,3,24,896]{3,2,1,0:T(8,128)(2,1)S(1)}, u32[]{:S(2)}, u32[]{:S(2)}) async-start(bf16[8,3,24,896]{3,2,1,0:T(8,128)(2,1)} %get-tuple-element.75), calls=%async_computation.2 | async-start | bytes 2064384 | tf_op jit(solution)/shard_map/all_to_all | solution.py:336
  147.2 8.9 %shard_map.90 = (bf16[8,5,24,896]{3,2,1,0:T(8,128)(2,1)}, s32[3]{0:T(128)}) custom-call(s32[5]{0:T(128)S(1)} %get-tuple-element.76.place_ref, s32[1]{0:T(128)} %bitcast.1.core_ref, s32[3]{0:T(128)S(1)} %and_select_fusion.1.place_ref.next_ref, bf16[1024,896]{1,0:T(8,128)(2,1)S(1)} %bitcast.25, bf16[1024,896]{1,0:T(8,128)(2,1)} %collective-permute-done.9.mate_ref, ...), custom_call_target="tpu_custom_call" | custom-call | tf_op jit(solution)/shard_map/pallas_call | solution.py:130
  156.2 5.3 %all-to-all-done.2.back_ref = bf16[8,3,24,896]{3,2,1,0:T(8,128)(2,1)S(1)} async-done(((bf16[8,3,24,896]{3,2,1,0:T(8,128)(2,1)}), bf16[8,3,24,896]{3,2,1,0:T(8,128)(2,1)S(1)}, u32[]{:S(2)}, u32[]{:S(2)}) %all-to-all-start.2) | async-done | bytes 1032224 | tf_op jit(solution)/shard_map/all_to_all | solution.py:336
  161.5 1.0 copy-done.4
  162.5 6.0 %all-to-all-start.3 = ((bf16[8,5,24,896]{3,2,1,0:T(8,128)(2,1)}), bf16[8,5,24,896]{3,2,1,0:T(8,128)(2,1)}, u32[]{:S(2)}, u32[]{:S(2)}) async-start(bf16[8,5,24,896]{3,2,1,0:T(8,128)(2,1)} %get-tuple-element.77), calls=%async_computation.3 | async-start | bytes 3440640 | tf_op jit(solution)/shard_map/all_to_all | solution.py:342
  168.4 0.1 add_select_fusion
  168.5 0.3 fusion.2
  168.8 2.5 %shard_map.91 = (bf16[128,896]{1,0:T(8,128)(2,1)}, bf16[128,896]{1,0:T(8,128)(2,1)}, bf16[128,896]{1,0:T(8,128)(2,1)}) custom-call(bf16[3,192,128]{2,1,0:T(8,128)(2,1)S(1)} %bitcast.29, bf16[8,3,24,896]{3,2,1,0:T(8,128)(2,1)} %copy-done.4), custom_call_target="tpu_custom_call" | custom-call | tf_op jit(solution)/shard_map/pallas_call | solution.py:228
  171.3 4.1 %collective-permute-start.14 = (bf16[128,896]{1,0:T(8,128)(2,1)}, bf16[128,896]{1,0:T(8,128)(2,1)S(1)}, u32[]{:S(2)}, u32[]{:S(2)}) collective-permute-start(bf16[128,896]{1,0:T(8,128)(2,1)} %get-tuple-element.79), channel_id=1, source_target_pairs={{0,4},{1,5},{2,6},{3,7},{4,0},{5,1},{6,2},{7,3},{8,12},{9,13},{10,... | collective-permute-start | bytes 688136 | tf_op jit(solution)/shard_map/ppermute | solution.py:32
  175.4 1.4 collective-permute-start.15
  176.8 3.6 %collective-permute-start.16 = (bf16[128,896]{1,0:T(8,128)(2,1)}, bf16[128,896]{1,0:T(8,128)(2,1)S(1)}, u32[]{:S(2)}, u32[]{:S(2)}) collective-permute-start(bf16[128,896]{1,0:T(8,128)(2,1)} %get-tuple-element.81), channel_id=1, source_target_pairs={{0,5},{1,6},{2,7},{3,0},{4,1},{5,2},{6,3},{7,4},{8,13},{9,14},{10,... | collective-permute-start | bytes 688136 | tf_op jit(solution)/shard_map/ppermute | solution.py:32
  180.4 11.7 %shard_map.92 = f32[896,1024]{1,0:T(8,128)} custom-call(s32[1]{0:T(128)} %bitcast.1.core_ref, bf16[8,192,2048]{2,1,0:T(8,128)(2,1)} %bitcast.39, bf16[8,192,2048]{2,1,0:T(8,128)(2,1)} %collective-permute-done.11.mate_values_ref, bf16[1536,896]{1,0:T(8,128)(2,1)S(1)} %bitcast.27, bf16[1536,896]{1,0:T(8,128)(2,1)} %collective-permute-done.12.mate_ref), custom_call_target="tpu_custom_call" | custom-call | tf_op jit(solution)/shard_map/pallas_call | solution.py:169
  192.1 2.2 abs_reduce_fusion
  195.0 2.2 collective-permute-start.13
  197.3 0.2 collective-permute-done.15.refs_2_
  197.4 3.2 %collective-permute-done.16.refs_1_ = bf16[128,896]{1,0:T(8,128)(2,1)S(1)} collective-permute-done((bf16[128,896]{1,0:T(8,128)(2,1)}, bf16[128,896]{1,0:T(8,128)(2,1)S(1)}, u32[]{:S(2)}, u32[]{:S(2)}) %collective-permute-start.16) | collective-permute-done | bytes 229408 | tf_op jit(solution)/shard_map/ppermute | solution.py:32
  200.6 2.7 %dynamic-slice_bitcast_fusion = (f32[448,1024]{1,0:T(8,128)S(1)}, f16[448,1024]{1,0:T(8,128)(2,1)S(1)}) fusion(f32[2,448,1024]{2,1,0:T(8,128)} %bitcast.41, s32[]{:T(128)S(6)} %select_n.84, f32[]{:T(128)} %bitcast.15, s32[]{:T(128)S(6)} %select_n.83), kind=kLoop, calls=%fused_computation.2 | loop fusion | flops 917504 | bytes 6422540 | tf_op jit(solution)/shard_map/jit(dynamic_index_in_dim)/squeeze | solution.py:347
  203.3 2.4 %collective-permute-start.17 = (f16[448,1024]{1,0:T(8,128)(2,1)S(1)}, f16[448,1024]{1,0:T(8,128)(2,1)S(1)}, u32[]{:S(2)}, u32[]{:S(2)}) collective-permute-start(f16[448,1024]{1,0:T(8,128)(2,1)S(1)} %get-tuple-element.86), channel_id=1, source_target_pairs={{0,8},{8,0},{1,9},{9,1},{2,10},{10,2},{3,11},{11,3},{4,12},{12,4},... | collective-permute-start | bytes 2752520 | tf_op jit(solution)/shard_map/ppermute | solution.py:352
  205.7 2.0 shard_map.93
  207.7 0.6 collective-permute-start.18
  208.3 2.4 %collective-permute-start.19 = (bf16[128,896]{1,0:T(8,128)(2,1)S(1)}, bf16[128,896]{1,0:T(8,128)(2,1)S(1)}, u32[]{:S(2)}, u32[]{:S(2)}) collective-permute-start(bf16[128,896]{1,0:T(8,128)(2,1)S(1)} %get-tuple-element.90), channel_id=1, source_target_pairs={{0,2},{1,3},{2,4},{3,5},{4,6},{5,7},{6,0},{7,1},{8,10},{9,11},{10,... | collective-permute-start | bytes 688136 | tf_op jit(solution)/shard_map/ppermute | solution.py:32
  210.7 3.3 %collective-permute-start.20 = (bf16[128,896]{1,0:T(8,128)(2,1)S(1)}, bf16[128,896]{1,0:T(8,128)(2,1)S(1)}, u32[]{:S(2)}, u32[]{:S(2)}) collective-permute-start(bf16[128,896]{1,0:T(8,128)(2,1)S(1)} %get-tuple-element.91), channel_id=1, source_target_pairs={{0,7},{1,0},{2,1},{3,2},{4,3},{5,4},{6,5},{7,6},{8,15},{9,8},{10,9... | collective-permute-start | bytes 688136 | tf_op jit(solution)/shard_map/ppermute | solution.py:32
  214.0 9.6 %collective-permute-done.17 = f16[448,1024]{1,0:T(8,128)(2,1)S(1)} collective-permute-done((f16[448,1024]{1,0:T(8,128)(2,1)S(1)}, f16[448,1024]{1,0:T(8,128)(2,1)S(1)}, u32[]{:S(2)}, u32[]{:S(2)}) %collective-permute-start.17) | collective-permute-done | bytes 917536 | tf_op jit(solution)/shard_map/ppermute | solution.py:352
  223.6 2.3 multiply_add_fusion
  225.9 1.4 collective-permute-done.21.refs_6_
  227.3 1.8 shard_map.94
  (54 shorter events, 0.8 us)
Async XLA Ops:
  7.2 0.7 copy-start
  7.2 11.3 %copy-start.2 = (bf16[128,7168]{1,0:T(8,128)(2,1)S(1)}, bf16[128,7168]{1,0:T(8,128)(2,1)}, u32[]{:S(2)}) copy-start(bf16[128,7168]{1,0:T(8,128)(2,1)} %hidden_ref.1) | copy-start | bytes 5505028
  8.1 1.0 copy-start.3
  10.9 19.1 %copy-start.8 = (f32[1,448]{1,0:T(1,128)S(1)}, f32[1,448]{1,0:T(1,128)}, u32[]{:S(2)}) copy-start(f32[1,448]{1,0:T(1,128)} %param.10) | copy-start | bytes 5380
  10.9 19.1 %all-to-all-start = ((bf16[8,24,2048]{2,1,0:T(8,128)(2,1)}), bf16[8,24,2048]{2,1,0:T(8,128)(2,1)}, u32[]{:S(2)}, u32[]{:S(2)}) async-start(bf16[8,24,2048]{2,1,0:T(8,128)(2,1)} %shard_map.86), calls=%async_computation | async-start | bytes 1572864 | tf_op jit(solution)/shard_map/all_to_all | solution.py:288
  18.4 115.6 %all-gather.2.cloned.1.call-start = ((), (), s32[]{:S(2)}) async-start(), calls=%async_computation.4 | async-start | bytes 7077888 | tf_op jit(solution)/shard_map/all_gather | solution.py:296
  18.9 11.0 %collective-permute-start = (bf16[128,896]{1,0:T(8,128)(2,1)S(1)}, bf16[128,896]{1,0:T(8,128)(2,1)S(1)}, u32[]{:S(2)}, u32[]{:S(2)}) collective-permute-start(bf16[128,896]{1,0:T(8,128)(2,1)S(1)} %get-tuple-element.48), channel_id=1, source_target_pairs={{0,1},{1,2},{2,3},{3,4},{4,5},{5,6},{6,7},{7,0},{8,9},{9,10},{10,1... | collective-permute-start | bytes 688136 | tf_op jit(solution)/shard_map/ppermute | solution.py:32
  20.9 9.0 %collective-permute-start.1 = (bf16[128,896]{1,0:T(8,128)(2,1)S(1)}, bf16[128,896]{1,0:T(8,128)(2,1)S(1)}, u32[]{:S(2)}, u32[]{:S(2)}) collective-permute-start(bf16[128,896]{1,0:T(8,128)(2,1)S(1)} %get-tuple-element.49), channel_id=1, source_target_pairs={{0,7},{1,0},{2,1},{3,2},{4,3},{5,4},{6,5},{7,6},{8,15},{9,8},{10,9... | collective-permute-start | bytes 688136 | tf_op jit(solution)/shard_map/ppermute | solution.py:32
  30.0 14.1 %collective-permute-start.3 = (f32[448]{0:T(512)S(1)}, f32[448]{0:T(512)S(1)}, u32[]{:S(2)}, u32[]{:S(2)}) collective-permute-start(f32[448]{0:T(512)S(1)} %bitcast.45), channel_id=1, source_target_pairs={{0,8},{8,0},{1,9},{9,1},{2,10},{10,2},{3,11},{11,3},{4,12},{12,4},... | collective-permute-start | bytes 5384 | tf_op jit(solution)/shard_map/ppermute | solution.py:284
  30.9 55.9 %collective-permute-start.2 = (bf16[448,1024]{1,0:T(8,128)(2,1)}, bf16[448,1024]{1,0:T(8,128)(2,1)}, u32[]{:S(2)}, u32[]{:S(2)}) collective-permute-start(bf16[448,1024]{1,0:T(8,128)(2,1)} %bitcast.44), channel_id=1, source_target_pairs={{0,8},{8,0},{1,9},{9,1},{2,10},{10,2},{3,11},{11,3},{4,12},{12,4},... | collective-permute-start | bytes 2752520 | tf_op jit(solution)/shard_map/ppermute | solution.py:284
  32.1 22.2 %collective-permute-start.4 = (bf16[128,896]{1,0:T(8,128)(2,1)S(1)}, bf16[128,896]{1,0:T(8,128)(2,1)S(1)}, u32[]{:S(2)}, u32[]{:S(2)}) collective-permute-start(bf16[128,896]{1,0:T(8,128)(2,1)S(1)} %get-tuple-element.51), channel_id=1, source_target_pairs={{0,4},{1,5},{2,6},{3,7},{4,0},{5,1},{6,2},{7,3},{8,12},{9,13},{10,... | collective-permute-start | bytes 688136 | tf_op jit(solution)/shard_map/ppermute | solution.py:32
  39.3 36.1 %collective-permute-start.5 = (bf16[128,896]{1,0:T(8,128)(2,1)S(1)}, bf16[128,896]{1,0:T(8,128)(2,1)S(1)}, u32[]{:S(2)}, u32[]{:S(2)}) collective-permute-start(bf16[128,896]{1,0:T(8,128)(2,1)S(1)} %get-tuple-element.52), channel_id=1, source_target_pairs={{0,5},{1,6},{2,7},{3,0},{4,1},{5,2},{6,3},{7,4},{8,13},{9,14},{10,... | collective-permute-start | bytes 688136 | tf_op jit(solution)/shard_map/ppermute | solution.py:32
  39.3 36.1 %collective-permute-start.6 = (bf16[128,896]{1,0:T(8,128)(2,1)S(1)}, bf16[128,896]{1,0:T(8,128)(2,1)S(1)}, u32[]{:S(2)}, u32[]{:S(2)}) collective-permute-start(bf16[128,896]{1,0:T(8,128)(2,1)S(1)} %get-tuple-element.53), channel_id=1, source_target_pairs={{0,3},{1,4},{2,5},{3,6},{4,7},{5,0},{6,1},{7,2},{8,11},{9,12},{10,... | collective-permute-start | bytes 688136 | tf_op jit(solution)/shard_map/ppermute | solution.py:32
  44.1 37.9 %collective-permute-start.7 = (bf16[128,896]{1,0:T(8,128)(2,1)S(1)}, bf16[128,896]{1,0:T(8,128)(2,1)S(1)}, u32[]{:S(2)}, u32[]{:S(2)}) collective-permute-start(bf16[128,896]{1,0:T(8,128)(2,1)S(1)} %get-tuple-element.54), channel_id=1, source_target_pairs={{0,6},{1,7},{2,0},{3,1},{4,2},{5,3},{6,4},{7,5},{8,14},{9,15},{10,... | collective-permute-start | bytes 688136 | tf_op jit(solution)/shard_map/ppermute | solution.py:32
  54.3 32.5 %collective-permute-start.8 = (bf16[128,896]{1,0:T(8,128)(2,1)S(1)}, bf16[128,896]{1,0:T(8,128)(2,1)S(1)}, u32[]{:S(2)}, u32[]{:S(2)}) collective-permute-start(bf16[128,896]{1,0:T(8,128)(2,1)S(1)} %get-tuple-element.55), channel_id=1, source_target_pairs={{0,2},{1,3},{2,4},{3,5},{4,6},{5,7},{6,0},{7,1},{8,10},{9,11},{10,... | collective-permute-start | bytes 688136 | tf_op jit(solution)/shard_map/ppermute | solution.py:32
  89.2 6.1 %copy-start.7 = (bf16[1,448,1024]{2,1,0:T(8,128)(2,1)S(1)}, bf16[1,448,1024]{2,1,0:T(8,128)(2,1)}, u32[]{:S(2)}) copy-start(bf16[1,448,1024]{2,1,0:T(8,128)(2,1)} %param.9) | copy-start | bytes 2752516
  89.2 36.7 %all-to-all-start.1 = ((bf16[8,8,24,896]{3,2,1,0:T(8,128)(2,1)}), bf16[8,8,24,896]{3,2,1,0:T(8,128)(2,1)}, u32[]{:S(2)}, u32[]{:S(2)}) async-start(bf16[8,8,24,896]{3,2,1,0:T(8,128)(2,1)} %shard_map.88), calls=%async_computation.1 | async-start | bytes 5505024 | tf_op jit(solution)/shard_map/all_to_all | solution.py:312
  101.6 27.9 %collective-permute-start.9 = (bf16[1024,896]{1,0:T(8,128)(2,1)S(1)}, bf16[1024,896]{1,0:T(8,128)(2,1)}, u32[]{:S(2)}, u32[]{:S(2)}) collective-permute-start(bf16[1024,896]{1,0:T(8,128)(2,1)S(1)} %bitcast.23), channel_id=1, source_target_pairs={{0,16},{16,0},{1,17},{17,1},{2,18},{18,2},{3,19},{19,3},{4,20},{20... | collective-permute-start | bytes 5505032 | tf_op jit(solution)/shard_map/ppermute | solution.py:310
  101.8 27.6 %collective-permute-start.10 = (f32[1,896]{1,0:T(1,128)S(1)}, f32[1,896]{1,0:T(1,128)S(1)}, u32[]{:S(2)}, u32[]{:S(2)}) collective-permute-start(f32[1,896]{1,0:T(1,128)S(1)} %select_n.79.own_scales), channel_id=1, source_target_pairs={{0,16},{16,0},{1,17},{17,1},{2,18},{18,2},{3,19},{19,3},{4,20},{20... | collective-permute-start | bytes 10760 | tf_op jit(solution)/shard_map/ppermute | solution.py:310
  125.8 8.7 %copy-start.10 = (s32[3]{0:T(128)S(1)}, s32[3]{0:T(128)}, u32[]{:S(2)}) copy-start(s32[3]{0:T(128)} %constant.80.clone) | copy-start | bytes 40
  125.8 8.7 %copy-start.9 = (s32[5]{0:T(128)S(1)}, s32[5]{0:T(128)}, u32[]{:S(2)}) copy-start(s32[5]{0:T(128)} %constant.81.clone) | copy-start | bytes 64
  134.0 46.4 %collective-permute-start.11 = (bf16[8,192,2048]{2,1,0:T(8,128)(2,1)}, bf16[8,192,2048]{2,1,0:T(8,128)(2,1)}, u32[]{:S(2)}, u32[]{:S(2)}) collective-permute-start(bf16[8,192,2048]{2,1,0:T(8,128)(2,1)} %bitcast.30), channel_id=1, source_target_pairs={{0,16},{16,0},{1,17},{17,1},{2,18},{18,2},{3,19},{19,3},{4,20},{20... | collective-permute-start | bytes 18874376 | tf_op jit(solution)/shard_map/ppermute | solution.py:335
  134.1 46.3 %collective-permute-start.12 = (bf16[1536,896]{1,0:T(8,128)(2,1)}, bf16[1536,896]{1,0:T(8,128)(2,1)}, u32[]{:S(2)}, u32[]{:S(2)}) collective-permute-start(bf16[1536,896]{1,0:T(8,128)(2,1)} %bitcast.26), channel_id=1, source_target_pairs={{0,16},{16,0},{1,17},{17,1},{2,18},{18,2},{3,19},{19,3},{4,20},{20... | collective-permute-start | bytes 8257544 | tf_op jit(solution)/shard_map/ppermute | solution.py:314
  141.2 20.3 %all-to-all-start.2 = ((bf16[8,3,24,896]{3,2,1,0:T(8,128)(2,1)}), bf16[8,3,24,896]{3,2,1,0:T(8,128)(2,1)S(1)}, u32[]{:S(2)}, u32[]{:S(2)}) async-start(bf16[8,3,24,896]{3,2,1,0:T(8,128)(2,1)} %get-tuple-element.75), calls=%async_computation.2 | async-start | bytes 2064384 | tf_op jit(solution)/shard_map/all_to_all | solution.py:336
  161.5 1.0 copy-start.4
  162.5 17.9 %copy-start.1 = (bf16[8,8,24,896]{3,2,1,0:T(8,128)(2,1)S(1)}, bf16[8,8,24,896]{3,2,1,0:T(8,128)(2,1)}, u32[]{:S(2)}) copy-start(bf16[8,8,24,896]{3,2,1,0:T(8,128)(2,1)} %copy.16) | copy-start | bytes 8257540
  162.5 38.1 %all-to-all-start.3 = ((bf16[8,5,24,896]{3,2,1,0:T(8,128)(2,1)}), bf16[8,5,24,896]{3,2,1,0:T(8,128)(2,1)}, u32[]{:S(2)}, u32[]{:S(2)}) async-start(bf16[8,5,24,896]{3,2,1,0:T(8,128)(2,1)} %get-tuple-element.77), calls=%async_computation.3 | async-start | bytes 3440640 | tf_op jit(solution)/shard_map/all_to_all | solution.py:342
  168.8 8.0 %copy-start.5 = (bf16[8,8,24,128]{3,2,1,0:T(8,128)(2,1)}, bf16[8,8,24,128]{3,2,1,0:T(8,128)(2,1)S(1)}, u32[]{:S(2)}) copy-start(bf16[8,8,24,128]{3,2,1,0:T(8,128)(2,1)S(1)} %fusion.2) | copy-start | bytes 1179652
  171.3 25.9 %collective-permute-start.14 = (bf16[128,896]{1,0:T(8,128)(2,1)}, bf16[128,896]{1,0:T(8,128)(2,1)S(1)}, u32[]{:S(2)}, u32[]{:S(2)}) collective-permute-start(bf16[128,896]{1,0:T(8,128)(2,1)} %get-tuple-element.79), channel_id=1, source_target_pairs={{0,4},{1,5},{2,6},{3,7},{4,0},{5,1},{6,2},{7,3},{8,12},{9,13},{10,... | collective-permute-start | bytes 688136 | tf_op jit(solution)/shard_map/ppermute | solution.py:32
  175.4 22.1 %collective-permute-start.15 = (bf16[128,896]{1,0:T(8,128)(2,1)}, bf16[128,896]{1,0:T(8,128)(2,1)S(1)}, u32[]{:S(2)}, u32[]{:S(2)}) collective-permute-start(bf16[128,896]{1,0:T(8,128)(2,1)} %get-tuple-element.80), channel_id=1, source_target_pairs={{0,3},{1,4},{2,5},{3,6},{4,7},{5,0},{6,1},{7,2},{8,11},{9,12},{10,... | collective-permute-start | bytes 688136 | tf_op jit(solution)/shard_map/ppermute | solution.py:32
  176.8 23.8 %collective-permute-start.16 = (bf16[128,896]{1,0:T(8,128)(2,1)}, bf16[128,896]{1,0:T(8,128)(2,1)S(1)}, u32[]{:S(2)}, u32[]{:S(2)}) collective-permute-start(bf16[128,896]{1,0:T(8,128)(2,1)} %get-tuple-element.81), channel_id=1, source_target_pairs={{0,5},{1,6},{2,7},{3,0},{4,1},{5,2},{6,3},{7,4},{8,13},{9,14},{10,... | collective-permute-start | bytes 688136 | tf_op jit(solution)/shard_map/ppermute | solution.py:32
  195.0 8.3 %collective-permute-start.13 = (f32[1]{0:T(128)}, f32[1]{0:T(128)}, u32[]{:S(2)}, u32[]{:S(2)}) collective-permute-start(f32[1]{0:T(128)} %bitcast.14), channel_id=1, source_target_pairs={{0,8},{8,0},{1,9},{9,1},{2,10},{10,2},{3,11},{11,3},{4,12},{12,4},... | collective-permute-start | bytes 20 | tf_op jit(solution)/shard_map/ppermute | solution.py:350
  200.6 5.1 %copy-start.6 = (bf16[8,8,24,128]{3,2,1,0:T(8,128)(2,1)S(1)}, bf16[8,8,24,128]{3,2,1,0:T(8,128)(2,1)}, u32[]{:S(2)}) copy-start(bf16[8,8,24,128]{3,2,1,0:T(8,128)(2,1)} %copy-done.5) | copy-start | bytes 1179652
  203.3 20.3 %collective-permute-start.17 = (f16[448,1024]{1,0:T(8,128)(2,1)S(1)}, f16[448,1024]{1,0:T(8,128)(2,1)S(1)}, u32[]{:S(2)}, u32[]{:S(2)}) collective-permute-start(f16[448,1024]{1,0:T(8,128)(2,1)S(1)} %get-tuple-element.86), channel_id=1, source_target_pairs={{0,8},{8,0},{1,9},{9,1},{2,10},{10,2},{3,11},{11,3},{4,12},{12,4},... | collective-permute-start | bytes 2752520 | tf_op jit(solution)/shard_map/ppermute | solution.py:352
  207.7 18.2 %collective-permute-start.18 = (bf16[128,896]{1,0:T(8,128)(2,1)S(1)}, bf16[128,896]{1,0:T(8,128)(2,1)S(1)}, u32[]{:S(2)}, u32[]{:S(2)}) collective-permute-start(bf16[128,896]{1,0:T(8,128)(2,1)S(1)} %get-tuple-element.89), channel_id=1, source_target_pairs={{0,6},{1,7},{2,0},{3,1},{4,2},{5,3},{6,4},{7,5},{8,14},{9,15},{10,... | collective-permute-start | bytes 688136 | tf_op jit(solution)/shard_map/ppermute | solution.py:32
  208.3 17.6 %collective-permute-start.19 = (bf16[128,896]{1,0:T(8,128)(2,1)S(1)}, bf16[128,896]{1,0:T(8,128)(2,1)S(1)}, u32[]{:S(2)}, u32[]{:S(2)}) collective-permute-start(bf16[128,896]{1,0:T(8,128)(2,1)S(1)} %get-tuple-element.90), channel_id=1, source_target_pairs={{0,2},{1,3},{2,4},{3,5},{4,6},{5,7},{6,0},{7,1},{8,10},{9,11},{10,... | collective-permute-start | bytes 688136 | tf_op jit(solution)/shard_map/ppermute | solution.py:32
  210.7 15.2 %collective-permute-start.20 = (bf16[128,896]{1,0:T(8,128)(2,1)S(1)}, bf16[128,896]{1,0:T(8,128)(2,1)S(1)}, u32[]{:S(2)}, u32[]{:S(2)}) collective-permute-start(bf16[128,896]{1,0:T(8,128)(2,1)S(1)} %get-tuple-element.91), channel_id=1, source_target_pairs={{0,7},{1,0},{2,1},{3,2},{4,3},{5,4},{6,5},{7,6},{8,15},{9,8},{10,9... | collective-permute-start | bytes 688136 | tf_op jit(solution)/shard_map/ppermute | solution.py:32
  214.0 13.3 %collective-permute-start.21 = (bf16[128,896]{1,0:T(8,128)(2,1)S(1)}, bf16[128,896]{1,0:T(8,128)(2,1)S(1)}, u32[]{:S(2)}, u32[]{:S(2)}) collective-permute-start(bf16[128,896]{1,0:T(8,128)(2,1)S(1)} %get-tuple-element.92), channel_id=1, source_target_pairs={{0,1},{1,2},{2,3},{3,4},{4,5},{5,6},{6,7},{7,0},{8,9},{9,10},{10,1... | collective-permute-start | bytes 688136 | tf_op jit(solution)/shard_map/ppermute | solution.py:32
Sparse Core Ops, SparseCore 0:
  30.1 103.8 all-gather.1

commit v2 on v0

--- a/solution.py
+++ b/solution.py
@@ -330,14 +330,14 @@
     send_home(order[:cut], far_back)
     own_hidden, mate_hidden = after((own_hidden, mate_hidden), *far_back)
     sums = weight_sums(core_word, values, mate_values, own_hidden, mate_hidden)
-    close_raw = after(lax.all_to_all(close_joined, PLACES, 0, 0), *came.values(), sums)
-    send_home(order[cut:], unpack(near_hot[cut:], close_raw))
-
     sums = sums.reshape(2, share, half)
     gone = lax.dynamic_index_in_dim(sums, 1 - side, 0, keepdims=False)
     kept = lax.dynamic_index_in_dim(sums, side, 0, keepdims=False)
     largest = jnp.maximum(jnp.max(jnp.abs(gone)), 1e-30).reshape(1)
     gone = (gone * (1 / largest)).astype(jnp.float16)
+    close_raw = after(lax.all_to_all(close_joined, PLACES, 0, 0), *came.values(), gone, kept)
+    send_home(order[cut:], unpack(near_hot[cut:], close_raw))
+
     largest = lax.ppermute(largest, "xl", SWAP)
     gone, kept, largest, _ = lax.optimization_barrier((gone, kept, largest, close_raw))
     gone = lax.ppermute(gone, "xl", SWAP)

time: 237 us -> 234 us (0.987)
  waiting for transfers between devices: 87.1 us -> 84 us
    ppermute x14, waiting for transfers between devices: 43.5 us -> 40.2 us  [along_z(): lax.ppermute(value, 'z', [(i, (i + by) % depth) for i in range(depth)])]
  transfers between devices with their start and end apart: 27 -> 27, of which waited for: 13 -> 11; matrix products, arithmetic and copies ran while one was open for 8% -> 8% of each run, Pallas kernels for 14% -> 14%
where the time goes in v2:
time: 234 us; the launch traced here: 233 us
  waiting for transfers between devices  84 us (36%)
  starting transfers between devices  74.4 us (32%)
  Pallas kernels  36.1 us (15%)
  between operations  15 us (6%)
  local copies, waits for them, and re-layouts  11.8 us (5%)
  other arithmetic  11.7 us (5%)
    ppermute x14, starting transfers between devices, along_z(): lax.ppermute(value, 'z', [(i, (i + by) % depth) for i in range(depth)])  42 us
    ppermute x14, waiting for transfers between devices, along_z(): lax.ppermute(value, 'z', [(i, (i + by) % depth) for i in range(depth)])  40.2 us
    all_to_all x1, waiting for transfers between devices, shards(): own_hidden = lax.all_to_all(hidden_slots, PLACES, 0, 0)  23.6 us
    pallas_call x2, Pallas kernels, join_rows(): pl.pallas_call(join_rows_kernel, out_shape=[pltpu.HBM(shape, jnp.bfloat16...  14.9 us
    pallas_call x1, Pallas kernels, weight_sums(): pl.pallas_call(weight_kernel, out_shape=pltpu.HBM((wide, half), jnp.float...  11.7 us
    ppermute x1, waiting for transfers between devices, shards(): gone = lax.ppermute(gone, 'xl', SWAP)  9.84 us
    all_to_all x1, starting transfers between devices, shards(): arrived = lax.all_to_all(packed, PLACES, 0, 0).reshape(places * slots, cols)  7.57 us
    all_to_all x1, starting transfers between devices, shards(): own_hidden = lax.all_to_all(hidden_slots, PLACES, 0, 0)  6.14 us
  transfers between devices with their start and end apart: 27, of which 11 were waited for; matrix products, arithmetic and copies ran while one was open for 8% of the time, Pallas kernels for 14%

profile of v2, /device:TPU:6, one launch (start us, length us, event | category | flops | bytes accessed | tf_op | source)
XLA Modules:
  0.0 233.1 jit_solution(2515580818943728884)
XLA Ops:
  7.2 0.7 copy-done
  7.9 0.2 dynamic-slice_reduce_fusion.counts_ref
  8.1 1.0 copy-done.5
  9.1 1.8 shard_map.86
  10.9 7.6 %all-to-all-start = ((bf16[8,24,2048]{2,1,0:T(8,128)(2,1)}), bf16[8,24,2048]{2,1,0:T(8,128)(2,1)}, u32[]{:S(2)}, u32[]{:S(2)}) async-start(bf16[8,24,2048]{2,1,0:T(8,128)(2,1)} %shard_map.86), calls=%async_computation | async-start | bytes 1572864 | tf_op jit(solution)/shard_map/all_to_all | solution.py:280
  18.4 0.5 shard_map.87
  18.9 2.0 collective-permute-start
  20.9 4.0 %collective-permute-start.1 = (bf16[128,896]{1,0:T(8,128)(2,1)S(1)}, bf16[128,896]{1,0:T(8,128)(2,1)S(1)}, u32[]{:S(2)}, u32[]{:S(2)}) collective-permute-start(bf16[128,896]{1,0:T(8,128)(2,1)S(1)} %get-tuple-element.49), channel_id=1, source_target_pairs={{0,7},{1,0},{2,1},{3,2},{4,3},{5,4},{6,5},{7,6},{8,15},{9,8},{10,9... | collective-permute-start | bytes 688136 | tf_op jit(solution)/shard_map/ppermute | solution.py:32
  25.0 5.0 %collective-permute-done.refs_6_ = bf16[128,896]{1,0:T(8,128)(2,1)S(1)} collective-permute-done((bf16[128,896]{1,0:T(8,128)(2,1)S(1)}, bf16[128,896]{1,0:T(8,128)(2,1)S(1)}, u32[]{:S(2)}, u32[]{:S(2)}) %collective-permute-start) | collective-permute-done | bytes 229408 | tf_op jit(solution)/shard_map/ppermute | solution.py:32
  30.0 0.9 collective-permute-start.3
  30.9 1.2 collective-permute-start.2
  32.1 7.2 %collective-permute-start.4 = (bf16[128,896]{1,0:T(8,128)(2,1)S(1)}, bf16[128,896]{1,0:T(8,128)(2,1)S(1)}, u32[]{:S(2)}, u32[]{:S(2)}) collective-permute-start(bf16[128,896]{1,0:T(8,128)(2,1)S(1)} %get-tuple-element.51), channel_id=1, source_target_pairs={{0,4},{1,5},{2,6},{3,7},{4,0},{5,1},{6,2},{7,3},{8,12},{9,13},{10,... | collective-permute-start | bytes 688136 | tf_op jit(solution)/shard_map/ppermute | solution.py:32
  39.3 3.8 %collective-permute-start.6 = (bf16[128,896]{1,0:T(8,128)(2,1)S(1)}, bf16[128,896]{1,0:T(8,128)(2,1)S(1)}, u32[]{:S(2)}, u32[]{:S(2)}) collective-permute-start(bf16[128,896]{1,0:T(8,128)(2,1)S(1)} %get-tuple-element.53), channel_id=1, source_target_pairs={{0,3},{1,4},{2,5},{3,6},{4,7},{5,0},{6,1},{7,2},{8,11},{9,12},{10,... | collective-permute-start | bytes 688136 | tf_op jit(solution)/shard_map/ppermute | solution.py:32
  43.2 0.1 pad_add_fusion
  43.4 0.1 fusion.5
  43.4 0.1 stack.23
  43.6 0.1 lt.66
  43.9 0.1 lt.71
  43.9 0.1 add.89
  44.0 0.1 add.90
  44.1 0.9 collective-permute-start.7
  45.1 9.3 %collective-permute-done.4.refs_0_ = bf16[128,896]{1,0:T(8,128)(2,1)S(1)} collective-permute-done((bf16[128,896]{1,0:T(8,128)(2,1)S(1)}, bf16[128,896]{1,0:T(8,128)(2,1)S(1)}, u32[]{:S(2)}, u32[]{:S(2)}) %collective-permute-start.4) | collective-permute-done | bytes 229408 | tf_op jit(solution)/shard_map/ppermute | solution.py:32
  54.3 7.7 %collective-permute-start.8 = (bf16[128,896]{1,0:T(8,128)(2,1)S(1)}, bf16[128,896]{1,0:T(8,128)(2,1)S(1)}, u32[]{:S(2)}, u32[]{:S(2)}) collective-permute-start(bf16[128,896]{1,0:T(8,128)(2,1)S(1)} %get-tuple-element.55), channel_id=1, source_target_pairs={{0,2},{1,3},{2,4},{3,5},{4,6},{5,7},{6,0},{7,1},{8,10},{9,11},{10,... | collective-permute-start | bytes 688136 | tf_op jit(solution)/shard_map/ppermute | solution.py:32
  62.1 0.3 fusion.1.hot_ref
  62.4 13.1 %collective-permute-done.5.refs_1_ = bf16[128,896]{1,0:T(8,128)(2,1)S(1)} collective-permute-done((bf16[128,896]{1,0:T(8,128)(2,1)S(1)}, bf16[128,896]{1,0:T(8,128)(2,1)S(1)}, u32[]{:S(2)}, u32[]{:S(2)}) %collective-permute-start.5) | collective-permute-done | bytes 229408 | tf_op jit(solution)/shard_map/ppermute | solution.py:32
  75.4 6.6 %collective-permute-done.7.refs_3_ = bf16[128,896]{1,0:T(8,128)(2,1)S(1)} collective-permute-done((bf16[128,896]{1,0:T(8,128)(2,1)S(1)}, bf16[128,896]{1,0:T(8,128)(2,1)S(1)}, u32[]{:S(2)}, u32[]{:S(2)}) %collective-permute-start.7) | collective-permute-done | bytes 229408 | tf_op jit(solution)/shard_map/ppermute | solution.py:32
  82.0 4.8 %collective-permute-done.8.refs_4_ = bf16[128,896]{1,0:T(8,128)(2,1)S(1)} collective-permute-done((bf16[128,896]{1,0:T(8,128)(2,1)S(1)}, bf16[128,896]{1,0:T(8,128)(2,1)S(1)}, u32[]{:S(2)}, u32[]{:S(2)}) %collective-permute-start.8) | collective-permute-done | bytes 229408 | tf_op jit(solution)/shard_map/ppermute | solution.py:32
  86.8 2.4 %shard_map.88 = bf16[8,8,24,896]{3,2,1,0:T(8,128)(2,1)} custom-call(s32[1]{0:T(128)} %bitcast.level_ref, bf16[8,192,128]{2,1,0:T(8,128)(2,1)S(1)} %fusion.1.hot_ref, bf16[128,896]{1,0:T(8,128)(2,1)S(1)} %collective-permute-done.4.refs_0_, bf16[128,896]{1,0:T(8,128)(2,1)S(1)} %collective-permute-done.5.refs_1_, ...), custom_call_target="tpu_custom_call" | custom-call | tf_op jit(solution)/shard_map/pallas_call | solution.py:242
  89.2 6.1 %all-to-all-start.1 = ((bf16[8,8,24,896]{3,2,1,0:T(8,128)(2,1)}), bf16[8,8,24,896]{3,2,1,0:T(8,128)(2,1)}, u32[]{:S(2)}, u32[]{:S(2)}) async-start(bf16[8,8,24,896]{3,2,1,0:T(8,128)(2,1)} %shard_map.88), calls=%async_computation.1 | async-start | bytes 5505024 | tf_op jit(solution)/shard_map/all_to_all | solution.py:304
  95.3 3.1 %maximum_select_fusion = bf16[2,448,1024]{2,1,0:T(8,128)(2,1)} fusion(bf16[1,448,1024]{2,1,0:T(8,128)(2,1)} %bitcast.6, bf16[1,448,1024]{2,1,0:T(8,128)(2,1)S(1)} %copy-done.8, pred[]{:T(512)S(6)} %eq.27), kind=kLoop, calls=%fused_computation | loop fusion | flops 2752512 | bytes 3670017 | tf_op jit(solution)/shard_map/jit(_where)/select_n | solution.py:298
  98.5 3.1 %copy.15 = bf16[896,1024]{0,1:T(8,128)(2,1)S(1)} copy(bf16[896,1024]{1,0:T(8,128)(2,1)} %bitcast.42) | data formatting | bytes 3670016 | tf_op jit(solution)/shard_map/jit(_where)/select_n | solution.py:298
  101.5 0.1 collective-permute-start.9
  101.6 0.1 select_n.79.own_scales
  101.7 0.5 collective-permute-start.10
  102.2 23.6 %all-to-all-done.1 = bf16[8,8,24,896]{3,2,1,0:T(8,128)(2,1)} async-done(((bf16[8,8,24,896]{3,2,1,0:T(8,128)(2,1)}), bf16[8,8,24,896]{3,2,1,0:T(8,128)(2,1)}, u32[]{:S(2)}, u32[]{:S(2)}) %all-to-all-start.1) | async-done | bytes 2752544 | tf_op jit(solution)/shard_map/all_to_all | solution.py:304
  125.9 3.6 %copy.16 = bf16[8,8,24,896]{3,2,1,0:T(8,128)(2,1)} copy(bf16[8,8,24,896]{3,2,0,1:T(8,128)(2,1)} %bitcast.10) | data formatting | bytes 5505024 | tf_op jit(solution)/shard_map/transpose | solution.py:305
  129.5 4.6 %all-gather.2.cloned.1.call-done = bf16[1536,2048]{1,0:T(8,128)(2,1)} async-done(((bf16[192,2048]{1,0:T(8,128)(2,1)}), bf16[1536,2048]{1,0:T(8,128)(2,1)}) %all-gather.2.cloned.1.call-update) | async-done | bytes 6291472 | tf_op jit(solution)/shard_map/all_gather | solution.py:288
  134.1 0.5 collective-permute-start.12
  134.6 6.3 %shard_map.89 = (bf16[8,3,24,896]{3,2,1,0:T(8,128)(2,1)}, s32[5]{0:T(128)S(1)}) custom-call(s32[3]{0:T(128)S(1)} %and_select_fusion.1.place_ref.next_ref, s32[1]{0:T(128)} %bitcast.1.core_ref, s32[5]{0:T(128)S(1)} %and_select_fusion.next_ref, bf16[1024,896]{1,0:T(8,128)(2,1)S(1)} %bitcast.24, bf16[1024,896]{1,0:T(8,128)(2,1)} %collective-permute-done.9.mate_ref, ...), custom_call_target="tpu_custom_call" | custom-call | tf_op jit(solution)/shard_map/pallas_call | solution.py:123
  140.9 6.1 %all-to-all-start.2 = ((bf16[8,3,24,896]{3,2,1,0:T(8,128)(2,1)}), bf16[8,3,24,896]{3,2,1,0:T(8,128)(2,1)S(1)}, u32[]{:S(2)}, u32[]{:S(2)}) async-start(bf16[8,3,24,896]{3,2,1,0:T(8,128)(2,1)} %get-tuple-element.75), calls=%async_computation.2 | async-start | bytes 2064384 | tf_op jit(solution)/shard_map/all_to_all | solution.py:328
  147.0 8.6 %shard_map.90 = (bf16[8,5,24,896]{3,2,1,0:T(8,128)(2,1)}, s32[3]{0:T(128)}) custom-call(s32[5]{0:T(128)S(1)} %get-tuple-element.76.place_ref, s32[1]{0:T(128)} %bitcast.1.core_ref, s32[3]{0:T(128)S(1)} %and_select_fusion.1.place_ref.next_ref, bf16[1024,896]{1,0:T(8,128)(2,1)S(1)} %bitcast.25, bf16[1024,896]{1,0:T(8,128)(2,1)} %collective-permute-done.9.mate_ref, ...), custom_call_target="tpu_custom_call" | custom-call | tf_op jit(solution)/shard_map/pallas_call | solution.py:123
  155.6 5.6 %all-to-all-done.2.back_ref = bf16[8,3,24,896]{3,2,1,0:T(8,128)(2,1)S(1)} async-done(((bf16[8,3,24,896]{3,2,1,0:T(8,128)(2,1)}), bf16[8,3,24,896]{3,2,1,0:T(8,128)(2,1)S(1)}, u32[]{:S(2)}, u32[]{:S(2)}) %all-to-all-start.2) | async-done | bytes 1032224 | tf_op jit(solution)/shard_map/all_to_all | solution.py:328
  161.2 1.0 copy-done.2
  162.2 6.0 %all-to-all-start.3 = ((bf16[8,5,24,896]{3,2,1,0:T(8,128)(2,1)}), bf16[8,5,24,896]{3,2,1,0:T(8,128)(2,1)}, u32[]{:S(2)}, u32[]{:S(2)}) async-start(bf16[8,5,24,896]{3,2,1,0:T(8,128)(2,1)} %get-tuple-element.77), calls=%async_computation.3 | async-start | bytes 3440640 | tf_op jit(solution)/shard_map/all_to_all | solution.py:338
  168.2 0.1 add_select_fusion
  168.3 0.3 fusion.2
  168.6 1.3 copy-done.3
  169.9 1.1 shard_map.91
  171.0 4.1 %collective-permute-start.14 = (bf16[128,896]{1,0:T(8,128)(2,1)}, bf16[128,896]{1,0:T(8,128)(2,1)S(1)}, u32[]{:S(2)}, u32[]{:S(2)}) collective-permute-start(bf16[128,896]{1,0:T(8,128)(2,1)} %get-tuple-element.79), channel_id=1, source_target_pairs={{0,4},{1,5},{2,6},{3,7},{4,0},{5,1},{6,2},{7,3},{8,12},{9,13},{10,... | collective-permute-start | bytes 688136 | tf_op jit(solution)/shard_map/ppermute | solution.py:32
  175.1 1.4 collective-permute-start.15
  176.5 3.6 %collective-permute-start.16 = (bf16[128,896]{1,0:T(8,128)(2,1)}, bf16[128,896]{1,0:T(8,128)(2,1)S(1)}, u32[]{:S(2)}, u32[]{:S(2)}) collective-permute-start(bf16[128,896]{1,0:T(8,128)(2,1)} %get-tuple-element.81), channel_id=1, source_target_pairs={{0,5},{1,6},{2,7},{3,0},{4,1},{5,2},{6,3},{7,4},{8,13},{9,14},{10,... | collective-permute-start | bytes 688136 | tf_op jit(solution)/shard_map/ppermute | solution.py:32
  180.1 11.7 %shard_map.92 = f32[896,1024]{1,0:T(8,128)} custom-call(s32[1]{0:T(128)} %bitcast.1.core_ref, bf16[8,192,2048]{2,1,0:T(8,128)(2,1)} %bitcast.39, bf16[8,192,2048]{2,1,0:T(8,128)(2,1)} %collective-permute-done.11.mate_values_ref, bf16[1536,896]{1,0:T(8,128)(2,1)S(1)} %bitcast.27, bf16[1536,896]{1,0:T(8,128)(2,1)} %collective-permute-done.12.mate_ref), custom_call_target="tpu_custom_call" | custom-call | tf_op jit(solution)/shard_map/pallas_call | solution.py:161
  191.9 2.2 abs_reduce_fusion
  194.7 2.2 collective-permute-start.13
  197.0 3.4 %dynamic-slice_bitcast_fusion = (f32[448,1024]{1,0:T(8,128)S(1)}, f16[448,1024]{1,0:T(8,128)(2,1)}) fusion(f32[2,448,1024]{2,1,0:T(8,128)} %bitcast.41, s32[]{:T(128)S(6)} %select_n.84, f32[]{:T(128)} %bitcast.15, s32[]{:T(128)S(6)} %select_n.83), kind=kLoop, calls=%fused_computation.2 | loop fusion | flops 917504 | bytes 6422540 | tf_op jit(solution)/shard_map/jit(dynamic_index_in_dim)/squeeze | solution.py:335
  200.5 1.3 collective-permute-start.17
  201.8 2.0 shard_map.93
  203.8 1.6 collective-permute-start.18
  205.4 1.4 collective-permute-start.19
  206.8 4.2 %collective-permute-start.20 = (bf16[128,896]{1,0:T(8,128)(2,1)S(1)}, bf16[128,896]{1,0:T(8,128)(2,1)S(1)}, u32[]{:S(2)}, u32[]{:S(2)}) collective-permute-start(bf16[128,896]{1,0:T(8,128)(2,1)S(1)} %get-tuple-element.91), channel_id=1, source_target_pairs={{0,7},{1,0},{2,1},{3,2},{4,3},{5,4},{6,5},{7,6},{8,15},{9,8},{10,9... | collective-permute-start | bytes 688136 | tf_op jit(solution)/shard_map/ppermute | solution.py:32
  211.0 9.8 %collective-permute-done.17 = f16[448,1024]{1,0:T(8,128)(2,1)S(1)} collective-permute-done((f16[448,1024]{1,0:T(8,128)(2,1)}, f16[448,1024]{1,0:T(8,128)(2,1)S(1)}, u32[]{:S(2)}, u32[]{:S(2)}) %collective-permute-start.17) | collective-permute-done | bytes 917536 | tf_op jit(solution)/shard_map/ppermute | solution.py:343
  220.8 2.1 multiply_add_fusion
  223.0 1.5 collective-permute-done.21.refs_6_
  224.5 1.8 shard_map.94
  (56 shorter events, 0.7 us)
Async XLA Ops:
  7.2 0.7 copy-start
  7.2 11.3 %copy-start.4 = (bf16[128,7168]{1,0:T(8,128)(2,1)S(1)}, bf16[128,7168]{1,0:T(8,128)(2,1)}, u32[]{:S(2)}) copy-start(bf16[128,7168]{1,0:T(8,128)(2,1)} %hidden_ref.1) | copy-start | bytes 5505028
  8.1 1.0 copy-start.5
  10.9 19.1 %copy-start.9 = (f32[1,448]{1,0:T(1,128)S(1)}, f32[1,448]{1,0:T(1,128)}, u32[]{:S(2)}) copy-start(f32[1,448]{1,0:T(1,128)} %param.10) | copy-start | bytes 5380
  10.9 19.1 %all-to-all-start = ((bf16[8,24,2048]{2,1,0:T(8,128)(2,1)}), bf16[8,24,2048]{2,1,0:T(8,128)(2,1)}, u32[]{:S(2)}, u32[]{:S(2)}) async-start(bf16[8,24,2048]{2,1,0:T(8,128)(2,1)} %shard_map.86), calls=%async_computation | async-start | bytes 1572864 | tf_op jit(solution)/shard_map/all_to_all | solution.py:280
  18.4 115.6 %all-gather.2.cloned.1.call-start = ((), (), s32[]{:S(2)}) async-start(), calls=%async_computation.4 | async-start | bytes 7077888 | tf_op jit(solution)/shard_map/all_gather | solution.py:288
  18.9 11.0 %collective-permute-start = (bf16[128,896]{1,0:T(8,128)(2,1)S(1)}, bf16[128,896]{1,0:T(8,128)(2,1)S(1)}, u32[]{:S(2)}, u32[]{:S(2)}) collective-permute-start(bf16[128,896]{1,0:T(8,128)(2,1)S(1)} %get-tuple-element.48), channel_id=1, source_target_pairs={{0,1},{1,2},{2,3},{3,4},{4,5},{5,6},{6,7},{7,0},{8,9},{9,10},{10,1... | collective-permute-start | bytes 688136 | tf_op jit(solution)/shard_map/ppermute | solution.py:32
  20.9 9.0 %collective-permute-start.1 = (bf16[128,896]{1,0:T(8,128)(2,1)S(1)}, bf16[128,896]{1,0:T(8,128)(2,1)S(1)}, u32[]{:S(2)}, u32[]{:S(2)}) collective-permute-start(bf16[128,896]{1,0:T(8,128)(2,1)S(1)} %get-tuple-element.49), channel_id=1, source_target_pairs={{0,7},{1,0},{2,1},{3,2},{4,3},{5,4},{6,5},{7,6},{8,15},{9,8},{10,9... | collective-permute-start | bytes 688136 | tf_op jit(solution)/shard_map/ppermute | solution.py:32
  30.0 14.1 %collective-permute-start.3 = (f32[448]{0:T(512)S(1)}, f32[448]{0:T(512)S(1)}, u32[]{:S(2)}, u32[]{:S(2)}) collective-permute-start(f32[448]{0:T(512)S(1)} %bitcast.45), channel_id=1, source_target_pairs={{0,8},{8,0},{1,9},{9,1},{2,10},{10,2},{3,11},{11,3},{4,12},{12,4},... | collective-permute-start | bytes 5384 | tf_op jit(solution)/shard_map/ppermute | solution.py:276
  30.9 55.9 %collective-permute-start.2 = (bf16[448,1024]{1,0:T(8,128)(2,1)}, bf16[448,1024]{1,0:T(8,128)(2,1)}, u32[]{:S(2)}, u32[]{:S(2)}) collective-permute-start(bf16[448,1024]{1,0:T(8,128)(2,1)} %bitcast.44), channel_id=1, source_target_pairs={{0,8},{8,0},{1,9},{9,1},{2,10},{10,2},{3,11},{11,3},{4,12},{12,4},... | collective-permute-start | bytes 2752520 | tf_op jit(solution)/shard_map/ppermute | solution.py:276
  32.1 22.2 %collective-permute-start.4 = (bf16[128,896]{1,0:T(8,128)(2,1)S(1)}, bf16[128,896]{1,0:T(8,128)(2,1)S(1)}, u32[]{:S(2)}, u32[]{:S(2)}) collective-permute-start(bf16[128,896]{1,0:T(8,128)(2,1)S(1)} %get-tuple-element.51), channel_id=1, source_target_pairs={{0,4},{1,5},{2,6},{3,7},{4,0},{5,1},{6,2},{7,3},{8,12},{9,13},{10,... | collective-permute-start | bytes 688136 | tf_op jit(solution)/shard_map/ppermute | solution.py:32
  39.3 36.1 %collective-permute-start.5 = (bf16[128,896]{1,0:T(8,128)(2,1)S(1)}, bf16[128,896]{1,0:T(8,128)(2,1)S(1)}, u32[]{:S(2)}, u32[]{:S(2)}) collective-permute-start(bf16[128,896]{1,0:T(8,128)(2,1)S(1)} %get-tuple-element.52), channel_id=1, source_target_pairs={{0,5},{1,6},{2,7},{3,0},{4,1},{5,2},{6,3},{7,4},{8,13},{9,14},{10,... | collective-permute-start | bytes 688136 | tf_op jit(solution)/shard_map/ppermute | solution.py:32
  39.3 36.1 %collective-permute-start.6 = (bf16[128,896]{1,0:T(8,128)(2,1)S(1)}, bf16[128,896]{1,0:T(8,128)(2,1)S(1)}, u32[]{:S(2)}, u32[]{:S(2)}) collective-permute-start(bf16[128,896]{1,0:T(8,128)(2,1)S(1)} %get-tuple-element.53), channel_id=1, source_target_pairs={{0,3},{1,4},{2,5},{3,6},{4,7},{5,0},{6,1},{7,2},{8,11},{9,12},{10,... | collective-permute-start | bytes 688136 | tf_op jit(solution)/shard_map/ppermute | solution.py:32
  44.1 37.9 %collective-permute-start.7 = (bf16[128,896]{1,0:T(8,128)(2,1)S(1)}, bf16[128,896]{1,0:T(8,128)(2,1)S(1)}, u32[]{:S(2)}, u32[]{:S(2)}) collective-permute-start(bf16[128,896]{1,0:T(8,128)(2,1)S(1)} %get-tuple-element.54), channel_id=1, source_target_pairs={{0,6},{1,7},{2,0},{3,1},{4,2},{5,3},{6,4},{7,5},{8,14},{9,15},{10,... | collective-permute-start | bytes 688136 | tf_op jit(solution)/shard_map/ppermute | solution.py:32
  54.3 32.5 %collective-permute-start.8 = (bf16[128,896]{1,0:T(8,128)(2,1)S(1)}, bf16[128,896]{1,0:T(8,128)(2,1)S(1)}, u32[]{:S(2)}, u32[]{:S(2)}) collective-permute-start(bf16[128,896]{1,0:T(8,128)(2,1)S(1)} %get-tuple-element.55), channel_id=1, source_target_pairs={{0,2},{1,3},{2,4},{3,5},{4,6},{5,7},{6,0},{7,1},{8,10},{9,11},{10,... | collective-permute-start | bytes 688136 | tf_op jit(solution)/shard_map/ppermute | solution.py:32
  89.2 6.1 %copy-start.8 = (bf16[1,448,1024]{2,1,0:T(8,128)(2,1)S(1)}, bf16[1,448,1024]{2,1,0:T(8,128)(2,1)}, u32[]{:S(2)}) copy-start(bf16[1,448,1024]{2,1,0:T(8,128)(2,1)} %param.9) | copy-start | bytes 2752516
  89.2 36.7 %all-to-all-start.1 = ((bf16[8,8,24,896]{3,2,1,0:T(8,128)(2,1)}), bf16[8,8,24,896]{3,2,1,0:T(8,128)(2,1)}, u32[]{:S(2)}, u32[]{:S(2)}) async-start(bf16[8,8,24,896]{3,2,1,0:T(8,128)(2,1)} %shard_map.88), calls=%async_computation.1 | async-start | bytes 5505024 | tf_op jit(solution)/shard_map/all_to_all | solution.py:304
  101.5 27.9 %collective-permute-start.9 = (bf16[1024,896]{1,0:T(8,128)(2,1)S(1)}, bf16[1024,896]{1,0:T(8,128)(2,1)}, u32[]{:S(2)}, u32[]{:S(2)}) collective-permute-start(bf16[1024,896]{1,0:T(8,128)(2,1)S(1)} %bitcast.23), channel_id=1, source_target_pairs={{0,16},{16,0},{1,17},{17,1},{2,18},{18,2},{3,19},{19,3},{4,20},{20... | collective-permute-start | bytes 5505032 | tf_op jit(solution)/shard_map/ppermute | solution.py:302
  101.7 27.7 %collective-permute-start.10 = (f32[1,896]{1,0:T(1,128)S(1)}, f32[1,896]{1,0:T(1,128)S(1)}, u32[]{:S(2)}, u32[]{:S(2)}) collective-permute-start(f32[1,896]{1,0:T(1,128)S(1)} %select_n.79.own_scales), channel_id=1, source_target_pairs={{0,16},{16,0},{1,17},{17,1},{2,18},{18,2},{3,19},{19,3},{4,20},{20... | collective-permute-start | bytes 10760 | tf_op jit(solution)/shard_map/ppermute | solution.py:302
  125.9 8.7 %copy-start.11 = (s32[3]{0:T(128)S(1)}, s32[3]{0:T(128)}, u32[]{:S(2)}) copy-start(s32[3]{0:T(128)} %constant.80.clone) | copy-start | bytes 40
  125.9 8.7 %copy-start.10 = (s32[5]{0:T(128)S(1)}, s32[5]{0:T(128)}, u32[]{:S(2)}) copy-start(s32[5]{0:T(128)} %constant.81.clone) | copy-start | bytes 64
  134.0 46.1 %collective-permute-start.11 = (bf16[8,192,2048]{2,1,0:T(8,128)(2,1)}, bf16[8,192,2048]{2,1,0:T(8,128)(2,1)}, u32[]{:S(2)}, u32[]{:S(2)}) collective-permute-start(bf16[8,192,2048]{2,1,0:T(8,128)(2,1)} %bitcast.30), channel_id=1, source_target_pairs={{0,16},{16,0},{1,17},{17,1},{2,18},{18,2},{3,19},{19,3},{4,20},{20... | collective-permute-start | bytes 18874376 | tf_op jit(solution)/shard_map/ppermute | solution.py:327
  134.1 46.0 %collective-permute-start.12 = (bf16[1536,896]{1,0:T(8,128)(2,1)}, bf16[1536,896]{1,0:T(8,128)(2,1)}, u32[]{:S(2)}, u32[]{:S(2)}) collective-permute-start(bf16[1536,896]{1,0:T(8,128)(2,1)} %bitcast.26), channel_id=1, source_target_pairs={{0,16},{16,0},{1,17},{17,1},{2,18},{18,2},{3,19},{19,3},{4,20},{20... | collective-permute-start | bytes 8257544 | tf_op jit(solution)/shard_map/ppermute | solution.py:306
  140.9 20.3 %all-to-all-start.2 = ((bf16[8,3,24,896]{3,2,1,0:T(8,128)(2,1)}), bf16[8,3,24,896]{3,2,1,0:T(8,128)(2,1)S(1)}, u32[]{:S(2)}, u32[]{:S(2)}) async-start(bf16[8,3,24,896]{3,2,1,0:T(8,128)(2,1)} %get-tuple-element.75), calls=%async_computation.2 | async-start | bytes 2064384 | tf_op jit(solution)/shard_map/all_to_all | solution.py:328
  161.2 1.0 copy-start.2
  162.2 17.9 %copy-start.1 = (bf16[8,8,24,896]{3,2,1,0:T(8,128)(2,1)S(1)}, bf16[8,8,24,896]{3,2,1,0:T(8,128)(2,1)}, u32[]{:S(2)}) copy-start(bf16[8,8,24,896]{3,2,1,0:T(8,128)(2,1)} %copy.16) | copy-start | bytes 8257540
  162.2 38.2 %all-to-all-start.3 = ((bf16[8,5,24,896]{3,2,1,0:T(8,128)(2,1)}), bf16[8,5,24,896]{3,2,1,0:T(8,128)(2,1)}, u32[]{:S(2)}, u32[]{:S(2)}) async-start(bf16[8,5,24,896]{3,2,1,0:T(8,128)(2,1)} %get-tuple-element.77), calls=%async_computation.3 | async-start | bytes 3440640 | tf_op jit(solution)/shard_map/all_to_all | solution.py:338
  168.5 8.0 %copy-start.6 = (bf16[8,8,24,128]{3,2,1,0:T(8,128)(2,1)}, bf16[8,8,24,128]{3,2,1,0:T(8,128)(2,1)S(1)}, u32[]{:S(2)}) copy-start(bf16[8,8,24,128]{3,2,1,0:T(8,128)(2,1)S(1)} %fusion.2) | copy-start | bytes 1179652
  168.6 1.3 copy-start.3
  171.0 29.4 %collective-permute-start.14 = (bf16[128,896]{1,0:T(8,128)(2,1)}, bf16[128,896]{1,0:T(8,128)(2,1)S(1)}, u32[]{:S(2)}, u32[]{:S(2)}) collective-permute-start(bf16[128,896]{1,0:T(8,128)(2,1)} %get-tuple-element.79), channel_id=1, source_target_pairs={{0,4},{1,5},{2,6},{3,7},{4,0},{5,1},{6,2},{7,3},{8,12},{9,13},{10,... | collective-permute-start | bytes 688136 | tf_op jit(solution)/shard_map/ppermute | solution.py:32
  175.1 25.4 %collective-permute-start.15 = (bf16[128,896]{1,0:T(8,128)(2,1)}, bf16[128,896]{1,0:T(8,128)(2,1)S(1)}, u32[]{:S(2)}, u32[]{:S(2)}) collective-permute-start(bf16[128,896]{1,0:T(8,128)(2,1)} %get-tuple-element.80), channel_id=1, source_target_pairs={{0,3},{1,4},{2,5},{3,6},{4,7},{5,0},{6,1},{7,2},{8,11},{9,12},{10,... | collective-permute-start | bytes 688136 | tf_op jit(solution)/shard_map/ppermute | solution.py:32
  176.5 23.9 %collective-permute-start.16 = (bf16[128,896]{1,0:T(8,128)(2,1)}, bf16[128,896]{1,0:T(8,128)(2,1)S(1)}, u32[]{:S(2)}, u32[]{:S(2)}) collective-permute-start(bf16[128,896]{1,0:T(8,128)(2,1)} %get-tuple-element.81), channel_id=1, source_target_pairs={{0,5},{1,6},{2,7},{3,0},{4,1},{5,2},{6,3},{7,4},{8,13},{9,14},{10,... | collective-permute-start | bytes 688136 | tf_op jit(solution)/shard_map/ppermute | solution.py:32
  194.7 5.7 %collective-permute-start.13 = (f32[1]{0:T(128)}, f32[1]{0:T(128)}, u32[]{:S(2)}, u32[]{:S(2)}) collective-permute-start(f32[1]{0:T(128)} %bitcast.14), channel_id=1, source_target_pairs={{0,8},{8,0},{1,9},{9,1},{2,10},{10,2},{3,11},{11,3},{4,12},{12,4},... | collective-permute-start | bytes 20 | tf_op jit(solution)/shard_map/ppermute | solution.py:341
  197.0 4.8 %copy-start.7 = (bf16[8,8,24,128]{3,2,1,0:T(8,128)(2,1)S(1)}, bf16[8,8,24,128]{3,2,1,0:T(8,128)(2,1)}, u32[]{:S(2)}) copy-start(bf16[8,8,24,128]{3,2,1,0:T(8,128)(2,1)} %copy-done.6) | copy-start | bytes 1179652
  200.5 20.3 %collective-permute-start.17 = (f16[448,1024]{1,0:T(8,128)(2,1)}, f16[448,1024]{1,0:T(8,128)(2,1)S(1)}, u32[]{:S(2)}, u32[]{:S(2)}) collective-permute-start(f16[448,1024]{1,0:T(8,128)(2,1)} %get-tuple-element.86), channel_id=1, source_target_pairs={{0,8},{8,0},{1,9},{9,1},{2,10},{10,2},{3,11},{11,3},{4,12},{12,4},... | collective-permute-start | bytes 2752520 | tf_op jit(solution)/shard_map/ppermute | solution.py:343
  203.8 19.1 %collective-permute-start.18 = (bf16[128,896]{1,0:T(8,128)(2,1)S(1)}, bf16[128,896]{1,0:T(8,128)(2,1)S(1)}, u32[]{:S(2)}, u32[]{:S(2)}) collective-permute-start(bf16[128,896]{1,0:T(8,128)(2,1)S(1)} %get-tuple-element.89), channel_id=1, source_target_pairs={{0,6},{1,7},{2,0},{3,1},{4,2},{5,3},{6,4},{7,5},{8,14},{9,15},{10,... | collective-permute-start | bytes 688136 | tf_op jit(solution)/shard_map/ppermute | solution.py:32
  205.4 17.6 %collective-permute-start.19 = (bf16[128,896]{1,0:T(8,128)(2,1)S(1)}, bf16[128,896]{1,0:T(8,128)(2,1)S(1)}, u32[]{:S(2)}, u32[]{:S(2)}) collective-permute-start(bf16[128,896]{1,0:T(8,128)(2,1)S(1)} %get-tuple-element.90), channel_id=1, source_target_pairs={{0,2},{1,3},{2,4},{3,5},{4,6},{5,7},{6,0},{7,1},{8,10},{9,11},{10,... | collective-permute-start | bytes 688136 | tf_op jit(solution)/shard_map/ppermute | solution.py:32
  206.8 16.1 %collective-permute-start.20 = (bf16[128,896]{1,0:T(8,128)(2,1)S(1)}, bf16[128,896]{1,0:T(8,128)(2,1)S(1)}, u32[]{:S(2)}, u32[]{:S(2)}) collective-permute-start(bf16[128,896]{1,0:T(8,128)(2,1)S(1)} %get-tuple-element.91), channel_id=1, source_target_pairs={{0,7},{1,0},{2,1},{3,2},{4,3},{5,4},{6,5},{7,6},{8,15},{9,8},{10,9... | collective-permute-start | bytes 688136 | tf_op jit(solution)/shard_map/ppermute | solution.py:32
  211.0 13.5 %collective-permute-start.21 = (bf16[128,896]{1,0:T(8,128)(2,1)S(1)}, bf16[128,896]{1,0:T(8,128)(2,1)S(1)}, u32[]{:S(2)}, u32[]{:S(2)}) collective-permute-start(bf16[128,896]{1,0:T(8,128)(2,1)S(1)} %get-tuple-element.92), channel_id=1, source_target_pairs={{0,1},{1,2},{2,3},{3,4},{4,5},{5,6},{6,7},{7,0},{8,9},{9,10},{10,1... | collective-permute-start | bytes 688136 | tf_op jit(solution)/shard_map/ppermute | solution.py:32
Sparse Core Ops, SparseCore 0:
  30.1 103.8 all-gather.1
